TPU v7x, 256 devices: a whole 4x4x8 slice. The times are simulated.
256 devices in a mesh: group: 16 (over z, core), dev: 16 (over x, y).
Axes of the slice: x: 4, y: 4, z: 8, core: 2. Of those that a mesh axis runs over, the one named last changes fastest.
Arguments:
- tiles: bfloat16 [18432, 5, 128, 128], P(('group', 'dev')), may hold values from 0.00029945374 to 0.029907227
- tile_col: int32 [18432, 5], P(('group', 'dev')), may hold values from 0 to 63
- strip_group: int32 [18432], P(('group', 'dev')), may hold values from 0 to 15, as said below
- strip_slot: int32 [18432], P(('group', 'dev')), may hold values from 0 to 15
- live_count: int32 [256], P(('group', 'dev')), may hold values from 36 to 72, as said below
- omega: bfloat16 [131072, 128], P(('group', 'dev')), may hold values from -40 to 40
- idf: float32 [524288], P(('group', 'dev')), may hold values from 0.4 to 20
Outputs:
- q_basis: float32 [524288, 128], P(('group', 'dev'))
- doc_factor: bfloat16 [128, 131072], P(None, ('group', 'dev'))
Inputs may be any that keep to these rules, and one draw needn't show every extreme that they name: `strip_group`: among the 72 strips of one device at most 6 name one group; in every draw one group is named by exactly 6 strips of every device. `live_count`: some device has all 72 strips live.
All inputs are finite; a program needn't handle non-finite values.
Results may differ from a plain program's by a relative error of at most 0.0034.
Values may be sent and summed in bfloat16 or wider, within the bound.
A program may use at most 128 MiB of HBM per device.

v0:
```python
import jax
import jax.numpy as jnp
from jax import lax
from jax.sharding import Mesh
from jax.sharding import PartitionSpec as P

GROUP = ("group_0", "group_1")
DEV = ("dev_0", "dev_1")
GROUP_DEV = ("group_0", "group_1", "dev_0", "dev_1")


def laid_out(pieces, dim):
    shape = list(pieces.shape[1:])
    shape[dim] *= pieces.shape[0]
    return jnp.moveaxis(pieces, 0, dim).reshape(shape)


def sent_to_all(value, axis):
    count = lax.axis_size(axis)
    return lax.all_to_all(
        jnp.broadcast_to(value[None], (count, *value.shape)), axis, 0, 0, tiled=True
    )


def gathered_copies(value, axis, dim):
    return laid_out(sent_to_all(value, axis), dim)


def in_blocks(value, dim, count):
    before, after = (value.shape[:dim], value.shape[dim + 1 :])
    return jnp.moveaxis(value.reshape(*before, count, -1, *after), dim, 0)


def summed_on_arrival(value, axis, dim):
    pieces = in_blocks(value, dim, lax.axis_size(axis))
    arrived = lax.all_to_all(pieces, axis, split_axis=0, concat_axis=0, tiled=True)
    return arrived.sum(axis=0)


def summed_rows(value, axes, dim):
    far, near = axes
    pieces = in_blocks(value, dim, lax.axis_size(far))
    nearer = summed_on_arrival(pieces, near, dim + 1)
    arrived = lax.all_to_all(nearer, far, split_axis=0, concat_axis=0, tiled=True)
    return arrived.sum(axis=0)


def filled_up(lines, count):
    spare = -len(lines) % count
    return jnp.pad(lines, [(0, spare)] + [(0, 0)] * (lines.ndim - 1))


def whole_of(value, axes, dim):
    far, near = axes
    pieces = sent_to_all(sent_to_all(value, far), near)
    return laid_out(pieces.swapaxes(0, 1).reshape(-1, *value.shape), dim)


def total_of(value, axes):
    lines = value.reshape(-1)
    own = summed_rows(filled_up(lines, lax.axis_size(axes[0]) * lax.axis_size(axes[1])), axes, 0)
    whole = whole_of(own, axes, 0)
    return whole[: len(lines)].reshape(value.shape)


def summed_rows_2(value, axes, dim):
    if not axes:
        return value
    nearer = lax.psum_scatter(value, axes[0], scatter_dimension=dim, tiled=True)
    return summed_rows_2(nearer, axes[1:], dim)


def on_device(tiles, tile_col, strip_group, strip_slot, live_count, omega, idf):
    n_group = lax.axis_size(GROUP)
    n_dev = lax.axis_size(DEV)
    strips = tiles.shape[0]
    tile_edge = tiles.shape[2]
    sketch_cols = omega.shape[1]
    owned_blocks = idf.shape[0] // tile_edge
    capacity = max(2, (4 * strips + 3 * n_group - 1) // (3 * n_group))
    alive_mask = (jnp.arange(strips) < live_count[0]).astype(jnp.float32)
    group_omega = gathered_copies(omega, DEV, 0)
    omega_blocks = group_omega.reshape(-1, tile_edge, sketch_cols)
    picked = omega_blocks[tile_col]
    partial_value = jnp.einsum("stij,stjk->sik", tiles, picked, preferred_element_type=jnp.float32)
    partial_value = partial_value * alive_mask[:, None, None]
    member = (strip_group[:, None] == jnp.arange(n_group)[None, :]).astype(jnp.int32)
    rank_in = jnp.sum((jnp.cumsum(member, axis=0) - member) * member, axis=1)
    position = strip_group * capacity + rank_in
    labels = jnp.where(alive_mask > 0, strip_slot, -1).astype(jnp.float32)
    outgoing = (
        jnp.zeros((n_group * capacity, tile_edge, sketch_cols), jnp.float32)
        .at[position]
        .set(partial_value)
    )
    out_labels = jnp.full((n_group * capacity,), -1.0, jnp.float32).at[position].set(labels)
    arrived, arrived_labels = (
        lax.all_to_all(
            outgoing.reshape(n_group, capacity, tile_edge, sketch_cols),
            GROUP,
            split_axis=0,
            concat_axis=0,
            tiled=True,
        ),
        lax.all_to_all(
            out_labels.reshape(n_group, capacity), GROUP, split_axis=0, concat_axis=0, tiled=True
        ),
    )
    slot_ids = arrived_labels.reshape(-1).astype(jnp.int32)
    chooser = (jnp.arange(owned_blocks)[:, None] == slot_ids[None, :]).astype(jnp.float32)
    owned_rows = jnp.einsum(
        "rs,sik->rik",
        chooser,
        arrived.reshape(-1, tile_edge, sketch_cols),
        precision=lax.Precision.HIGHEST,
        preferred_element_type=jnp.float32,
    )
    sketch = owned_rows.reshape(-1, sketch_cols) * idf[:, None]
    total_terms = idf.shape[0] * n_group * n_dev
    local_gram = lax.dot_general(
        sketch,
        sketch,
        (((0,), (0,)), ((), ())),
        precision=lax.Precision.HIGHEST,
        preferred_element_type=jnp.float32,
    )
    gram_matrix = total_of(local_gram, (("group_0", "group_1", "dev_0"), "dev_1")) / total_terms
    lower_factor = jnp.linalg.cholesky(gram_matrix)
    q_basis = jax.scipy.linalg.solve_triangular(lower_factor, sketch.T, lower=True).T
    weighted = (
        (idf[:, None] * q_basis).astype(jnp.bfloat16).reshape(owned_blocks, tile_edge, sketch_cols)
    )
    clipped = jnp.clip(slot_ids, 0, owned_blocks - 1)
    replies = jnp.where(
        (slot_ids >= 0)[:, None, None], weighted[clipped], jnp.zeros((), jnp.bfloat16)
    )
    returned = lax.all_to_all(
        replies.reshape(n_group, capacity, tile_edge, sketch_cols),
        GROUP,
        split_axis=0,
        concat_axis=0,
        tiled=True,
    )
    strip_q = returned.reshape(-1, tile_edge, sketch_cols)[position]
    strip_q = strip_q * alive_mask.astype(jnp.bfloat16)[:, None, None]
    contrib = jnp.einsum("sik,stij->stkj", strip_q, tiles, preferred_element_type=jnp.float32)
    col_blocks = n_dev * (omega.shape[0] // tile_edge)
    doc_part = jax.ops.segment_sum(
        contrib.reshape(-1, sketch_cols, tile_edge), tile_col.reshape(-1), num_segments=col_blocks
    )
    my_docs = summed_rows_2(doc_part, DEV, 0)
    doc_factor = jnp.transpose(my_docs, (1, 0, 2)).reshape(sketch_cols, -1).astype(jnp.bfloat16)
    return (q_basis, doc_factor)


def solution(mesh):
    torus = Mesh(mesh.devices.reshape(8, 2, 4, 4), ("group_0", "group_1", "dev_0", "dev_1"))
    in_specs = (
        P(GROUP_DEV, None, None, None),
        P(GROUP_DEV, None),
        P(GROUP_DEV),
        P(GROUP_DEV),
        P(GROUP_DEV),
        P(GROUP_DEV, None),
        P(GROUP_DEV),
    )
    out_specs = (P(GROUP_DEV, None), P(None, GROUP_DEV))
    return jax.shard_map(
        on_device, mesh=torus, in_specs=in_specs, out_specs=out_specs, check_vma=False
    )
```

profile of v0, /device:TPU:2, one launch (start us, length us, event | category | flops | bytes accessed | tf_op | source)
XLA Modules:
  0.0 599.7 jit_solution(6135584538626168954)
XLA Ops:
  7.2 2.7 broadcast_in_dim.40
  9.9 7.5 %all-to-all-start.1 = ((bf16[16,512,128]{2,1,0:T(8,128)(2,1)}), bf16[16,512,128]{2,1,0:T(8,128)(2,1)S(1)}, u32[]{:S(2)}, u32[]{:S(2)}) async-start(bf16[16,512,128]{2,1,0:T(8,128)(2,1)} %broadcast_in_dim.40), calls=%async_computation.1 | async-start | bytes 4194304 | tf_op jit(solution)/shard_map/all_to_all | solution.py:20
  18.0 0.1 copy.45
  18.1 0.1 reshape.133
  18.4 0.1 reduce_window_sum.11
  18.5 0.2 select_reduce_fusion.1
  18.7 0.8 scatter_custom_fusion
  19.5 0.7 all_to_all.31
  20.2 24.3 %all-to-all-done.1 = bf16[16,512,128]{2,1,0:T(8,128)(2,1)S(1)} async-done(((bf16[16,512,128]{2,1,0:T(8,128)(2,1)}), bf16[16,512,128]{2,1,0:T(8,128)(2,1)S(1)}, u32[]{:S(2)}, u32[]{:S(2)}) %all-to-all-start.1) | async-done | bytes 2097184 | tf_op jit(solution)/shard_map/all_to_all | solution.py:20
  44.5 8.6 %all-to-all-start = ((f32[16,1,6]{2,1,0:T(1,128)}), f32[16,1,6]{2,1,0:T(1,128)S(1)}, u32[]{:S(2)}, u32[]{:S(2)}) async-start(f32[16,1,6]{2,1,0:T(1,128)} %bitcast.1), calls=%async_computation | async-start | bytes 16384 | tf_op jit(solution)/shard_map/all_to_all | solution.py:105
  53.1 11.1 %gather_fusion = bf16[360,128,128]{2,1,0:T(8,128)(2,1)} fusion(bf16[64,128,128]{2,1,0:T(8,128)(2,1)S(1)} %bitcast.72, s32[1024]{0:T(1024)S(1)} %pad_clamp_fusion.2), kind=kCustom, calls=%fused_computation | custom fusion | bytes 23594400 | tf_op jit(solution)/shard_map/gather | solution.py:84
  64.2 11.8 %fusion.2 = f32[72,128,128]{1,2,0:T(8,128)} fusion(f32[72]{0:T(128)S(1)} %compare_convert_fusion, bf16[72,5,128,128]{3,2,1,0:T(8,128)(2,1)} %bitcast.73, bf16[72,5,128,128]{3,2,1,0:T(8,128)(2,1)} %param.7), kind=kOutput, calls=%fused_computation.9 | convolution fusion | flops 1511129088 | bytes 28311840 | tf_op jit(solution)/shard_map/stij,stjk->sik/dot_general | solution.py:85
  76.0 6.1 %copy.47 = f32[72,128,128]{2,1,0:T(8,128)} copy(f32[72,128,128]{1,2,0:T(8,128)} %fusion.2) | data formatting | bytes 9437184 | tf_op jit(solution)/shard_map/mul | solution.py:86
  82.1 3.4 broadcast_in_dim.39
  85.5 14.6 %scatter_fusion = f32[96,128,128]{2,1,0:T(8,128)} fusion(f32[96,128,128]{2,1,0:T(8,128)} %broadcast_in_dim.39, s32[72]{0:T(128)S(1)} %get-tuple-element.8, f32[72,128,128]{2,1,0:T(8,128)} %copy.47), kind=kCustom, calls=%fused_computation.4 | custom fusion | bytes 14156064 | tf_op jit(solution)/shard_map/scatter | solution.py:94
  100.1 7.4 %all-to-all-start.2 = ((f32[16,6,128,128]{3,2,1,0:T(8,128)}), f32[16,6,128,128]{3,2,1,0:T(8,128)}, u32[]{:S(2)}, u32[]{:S(2)}) async-start(f32[16,6,128,128]{3,2,1,0:T(8,128)} %bitcast.74), calls=%async_computation.2 | async-start | bytes 12582912 | tf_op jit(solution)/shard_map/all_to_all | solution.py:98
  107.5 0.1 copy.49
  107.8 0.1 convert_element_type.63
  107.9 138.9 %all-to-all-done.2 = f32[16,6,128,128]{3,2,1,0:T(8,128)} async-done(((f32[16,6,128,128]{3,2,1,0:T(8,128)}), f32[16,6,128,128]{3,2,1,0:T(8,128)}, u32[]{:S(2)}, u32[]{:S(2)}) %all-to-all-start.2) | async-done | bytes 6291488 | tf_op jit(solution)/shard_map/all_to_all | solution.py:98
  246.8 8.3 %fusion.6 = f32[16,128,128]{2,0,1:T(8,128)S(1)} fusion(f32[96,128,128]{2,1,0:T(8,128)} %bitcast.9, f32[16,128]{0,1:T(8,128)S(1)} %copy.49, s32[96]{0:T(128)S(1)} %convert_element_type.63), kind=kOutput, calls=%fused_computation.14 | convolution fusion | flops 302253568 | bytes 7348608 | tf_op jit(solution)/shard_map/rs,sik->rik/dot_general | solution.py:111
  255.1 1.8 convolution_bitcast_fusion
  256.9 0.1 reshape_reshape.7
  257.0 0.8 reshape.191
  257.8 3.3 all-to-all-start.3
  261.1 5.6 all-to-all-done.3
  266.7 0.5 broadcast.154
  267.2 0.8 reduce.7
  268.0 0.1 reshape.192
  268.1 0.6 reduce_sum.28
  268.8 8.9 %all-to-all-start.4 = ((f32[64,1,64]{2,1,0:T(1,128)}), f32[64,1,64]{2,1,0:T(1,128)S(1)}, u32[]{:S(2)}, u32[]{:S(2)}) async-start(f32[64,1,64]{2,1,0:T(1,128)} %bitcast.14), calls=%async_computation.4 | async-start | bytes 65536 | tf_op jit(solution)/shard_map/all_to_all | solution.py:44
  277.9 8.4 %all-to-all-done.4 = f32[64,1,64]{2,1,0:T(1,128)S(1)} async-done(((f32[64,1,64]{2,1,0:T(1,128)}), f32[64,1,64]{2,1,0:T(1,128)S(1)}, u32[]{:S(2)}, u32[]{:S(2)}) %all-to-all-start.4) | async-done | bytes 16416 | tf_op jit(solution)/shard_map/all_to_all | solution.py:44
  286.3 0.6 broadcast_in_dim.71
  287.0 5.5 all-to-all-start.5
  292.5 8.7 %all-to-all-done.5 = f32[64,1,64]{2,1,0:T(1,128)S(1)} async-done(((f32[64,1,64]{2,1,0:T(1,128)}), f32[64,1,64]{2,1,0:T(1,128)S(1)}, u32[]{:S(2)}, u32[]{:S(2)}) %all-to-all-start.5) | async-done | bytes 16416 | tf_op jit(solution)/shard_map/all_to_all | solution.py:20
  301.2 0.8 reshape.193
  301.9 3.5 all-to-all-start.6
  305.4 0.1 copy.55
  305.5 0.3 copy.50
  305.9 4.9 all-to-all-done.6
  310.8 0.8 reduce.8
  311.6 0.1 reshape.194
  311.9 0.1 div.21
  312.1 11.7 %cholesky.16 = f32[128,128]{1,0:T(8,128)S(1)} custom-call(f32[128,128]{1,0:T(8,128)S(1)} %fusion.13), custom_call_target="Cholesky" | custom-call | tf_op jit(solution)/shard_map/jit(cholesky)/cholesky | solution.py:128
  323.8 0.6 compare_reduce_fusion
  324.5 0.7 fusion.10
  325.1 9.8 %custom-call.7 = f32[1,128,128]{1,2,0:T(8,128)S(1)} custom-call(f32[1,128,128]{2,1,0:T(8,128)S(1)} %fusion.10), custom_call_target="InvertDiagBlocksLowerTriangular" | custom-call | tf_op jit(solution)/shard_map/jit(_solve_triangular)/triangular_solve | solution.py:129
  334.9 1.9 multiply_convert_fusion
  336.9 2.8 gather_fusion.1
  339.6 3.8 broadcast_select_fusion
  343.5 3.7 all-to-all-start.7
  347.2 0.3 reduce-scatter.3.cloned.1.call-start
  347.5 0.1 copy.54
  347.6 0.1 reshape.173
  347.8 71.1 %all-to-all-done.7 = bf16[16,6,128,128]{3,2,1,0:T(8,128)(2,1)S(1)} async-done(((bf16[16,6,128,128]{3,2,1,0:T(8,128)(2,1)}), bf16[16,6,128,128]{3,2,1,0:T(8,128)(2,1)S(1)}, u32[]{:S(2)}, u32[]{:S(2)}) %all-to-all-start.7) | async-done | bytes 3145760 | tf_op jit(solution)/shard_map/all_to_all | solution.py:137
  418.9 1.7 copy-done
  420.6 2.9 gather_fusion.2
  423.5 15.5 %fusion.3 = f32[72,128,5,128]{3,1,2,0:T(8,128)} fusion(bf16[72,5,128,128]{3,2,1,0:T(8,128)(2,1)} %param.7, bf16[72,128,128]{2,1,0:T(8,128)(2,1)S(1)} %gather_fusion.2, bf16[72]{0:T(256)(128)(2,1)S(1)} %fusion.22), kind=kOutput, calls=%fused_computation.11 | convolution fusion | flops 1514668032 | bytes 37748880 | tf_op jit(solution)/shard_map/sik,stij->stkj/dot_general | solution.py:146
  439.0 2.6 broadcast_in_dim.74
  441.5 74.8 %scatter_fusion.1 = f32[64,128,128]{2,1,0:T(8,128)} fusion(f32[64,128,128]{2,1,0:T(8,128)} %broadcast_in_dim.74, s32[360]{0:T(512)S(1)} %reshape.173, f32[360,128,128]{2,1,0:T(8,128)} %bitcast.71), kind=kCustom, calls=%fused_computation.5 | custom fusion | flops 5898240 | bytes 70780320 | tf_op jit(solution)/shard_map/scatter-add | solution.py:148
  516.4 44.7 %reduce-scatter.3.cloned.1.call-done = f32[16,128,128]{2,1,0:T(8,128)} async-done(((f32[64,128,128]{2,1,0:T(8,128)}), f32[16,128,128]{2,1,0:T(8,128)}) %reduce-scatter.3.cloned.1.call-update) | async-done | bytes 1048592 | tf_op jit(solution)/shard_map/reduce_scatter | solution.py:69
  561.1 29.8 %reduce-scatter.5.cloned.1.call-done = f32[4,128,128]{2,1,0:T(8,128)} async-done(((f32[16,128,128]{2,1,0:T(8,128)}), f32[4,128,128]{2,1,0:T(8,128)}) %reduce-scatter.5.cloned.1.call-update) | async-done | bytes 262160 | tf_op jit(solution)/shard_map/reduce_scatter | solution.py:69
  590.9 1.0 convert_bitcast_fusion
  591.9 0.1 copy.58
  592.0 0.8 copy.59
  (37 shorter events, 0.9 us)
Async XLA Ops:
  7.2 10.8 %copy-start.2 = (s32[72,5]{0,1:T(8,128)S(1)}, s32[72,5]{0,1:T(8,128)}, u32[]{:S(2)}) copy-start(s32[72,5]{0,1:T(8,128)} %param.8) | copy-start | bytes 4324
  7.2 11.1 %copy-start.3 = (s32[72]{0:T(128)S(1)}, s32[72]{0:T(128)}, u32[]{:S(2)}) copy-start(s32[72]{0:T(128)} %param.9) | copy-start | bytes 868
  7.2 11.5 %copy-start.4 = (s32[72]{0:T(128)S(1)}, s32[72]{0:T(128)}, u32[]{:S(2)}) copy-start(s32[72]{0:T(128)} %param.10) | copy-start | bytes 868
  9.9 34.6 %all-to-all-start.1 = ((bf16[16,512,128]{2,1,0:T(8,128)(2,1)}), bf16[16,512,128]{2,1,0:T(8,128)(2,1)S(1)}, u32[]{:S(2)}, u32[]{:S(2)}) async-start(bf16[16,512,128]{2,1,0:T(8,128)(2,1)} %broadcast_in_dim.40), calls=%async_computation.1 | async-start | bytes 4194304 | tf_op jit(solution)/shard_map/all_to_all | solution.py:20
  44.5 55.6 %all-to-all-start = ((f32[16,1,6]{2,1,0:T(1,128)}), f32[16,1,6]{2,1,0:T(1,128)S(1)}, u32[]{:S(2)}, u32[]{:S(2)}) async-start(f32[16,1,6]{2,1,0:T(1,128)} %bitcast.1), calls=%async_computation | async-start | bytes 16384 | tf_op jit(solution)/shard_map/all_to_all | solution.py:105
  100.1 7.4 %copy-start.1 = (f32[2048]{0:T(1024)S(1)}, f32[2048]{0:T(1024)}, u32[]{:S(2)}) copy-start(f32[2048]{0:T(1024)} %param.13) | copy-start | bytes 24580
  100.1 146.7 %all-to-all-start.2 = ((f32[16,6,128,128]{3,2,1,0:T(8,128)}), f32[16,6,128,128]{3,2,1,0:T(8,128)}, u32[]{:S(2)}, u32[]{:S(2)}) async-start(f32[16,6,128,128]{3,2,1,0:T(8,128)} %bitcast.74), calls=%async_computation.2 | async-start | bytes 12582912 | tf_op jit(solution)/shard_map/all_to_all | solution.py:98
  257.8 8.9 %all-to-all-start.3 = ((f32[4,1,4096]{2,1,0:T(1,128)}), f32[4,1,4096]{2,1,0:T(1,128)S(1)}, u32[]{:S(2)}, u32[]{:S(2)}) async-start(f32[4,1,4096]{2,1,0:T(1,128)} %reshape.191), calls=%async_computation.3 | async-start | bytes 131072 | tf_op jit(solution)/shard_map/all_to_all | solution.py:36
  268.8 17.5 %all-to-all-start.4 = ((f32[64,1,64]{2,1,0:T(1,128)}), f32[64,1,64]{2,1,0:T(1,128)S(1)}, u32[]{:S(2)}, u32[]{:S(2)}) async-start(f32[64,1,64]{2,1,0:T(1,128)} %bitcast.14), calls=%async_computation.4 | async-start | bytes 65536 | tf_op jit(solution)/shard_map/all_to_all | solution.py:44
  287.0 14.2 %all-to-all-start.5 = ((f32[64,1,64]{2,1,0:T(1,128)}), f32[64,1,64]{2,1,0:T(1,128)S(1)}, u32[]{:S(2)}, u32[]{:S(2)}) async-start(f32[64,1,64]{2,1,0:T(1,128)} %broadcast_in_dim.71), calls=%async_computation.5 | async-start | bytes 65536 | tf_op jit(solution)/shard_map/all_to_all | solution.py:20
  301.9 8.9 %all-to-all-start.6 = ((f32[4,1,4096]{2,1,0:T(1,128)}), f32[4,1,4096]{2,1,0:T(1,128)S(1)}, u32[]{:S(2)}, u32[]{:S(2)}) async-start(f32[4,1,4096]{2,1,0:T(1,128)} %reshape.193), calls=%async_computation.6 | async-start | bytes 131072 | tf_op jit(solution)/shard_map/all_to_all | solution.py:20
  343.5 75.5 %all-to-all-start.7 = ((bf16[16,6,128,128]{3,2,1,0:T(8,128)(2,1)}), bf16[16,6,128,128]{3,2,1,0:T(8,128)(2,1)S(1)}, u32[]{:S(2)}, u32[]{:S(2)}) async-start(bf16[16,6,128,128]{3,2,1,0:T(8,128)(2,1)} %broadcast_select_fusion), calls=%async_computation.7 | async-start | bytes 6291456 | tf_op jit(solution)/shard_map/all_to_all | solution.py:137
  347.2 213.8 %reduce-scatter.3.cloned.1.call-start = ((), (), s32[]{:S(2)}) async-start(), calls=%async_computation.10 | async-start | bytes 5242880 | tf_op jit(solution)/shard_map/reduce_scatter | solution.py:69
  418.9 1.7 copy-start
  516.3 74.6 %reduce-scatter.5.cloned.1.call-start = ((), (), s32[]{:S(2)}) async-start(), calls=%async_computation.11 | async-start | bytes 1310720 | tf_op jit(solution)/shard_map/reduce_scatter | solution.py:69
Sparse Core Ops, SparseCore 0:
  516.4 44.5 reduce-scatter.2
  563.8 27.0 reduce-scatter.4
where the time goes:
time: 601 us; the launch traced here: 600 us
  waiting for transfers between devices  336 us (56%)
  other arithmetic  105 us (17%)
  local copies, waits for them, and re-layouts  54.9 us (9%)
  starting transfers between devices  48.8 us (8%)
  matrix products  39.3 us (7%)
  between operations  15 us (2%)
    all_to_all x1, waiting for transfers between devices, on_device(): lax.all_to_all(outgoing.reshape(n_group, capacity, tile_edge, sketch_cols...  139 us
    scatter-add x1, other arithmetic, on_device(): jax.ops.segment_sum(contrib.reshape(-1, sketch_cols, tile_edge), tile_col...  74.8 us
    reduce_scatter x2, waiting for transfers between devices, summed_rows_2(): nearer = lax.psum_scatter(value, axes[0], scatter_dimension=dim, tiled=True)  74.5 us
    all_to_all x1, waiting for transfers between devices, on_device(): lax.all_to_all(replies.reshape(n_group, capacity, tile_edge, sketch_cols)...  71.1 us
    all_to_all x3, waiting for transfers between devices, sent_to_all(): lax.all_to_all(jnp.broadcast_to(value[None], (count, *value.shape)), axis...  37.9 us
    all_to_all x3, starting transfers between devices, sent_to_all(): lax.all_to_all(jnp.broadcast_to(value[None], (count, *value.shape)), axis...  16.5 us
    dot_general x1, matrix products, on_device(): jnp.einsum('sik,stij->stkj', strip_q, tiles, preferred_element_type=jnp.f...  15.5 us
    scatter x1, local copies, waits for them, and re-layouts, on_device(): outgoing = jnp.zeros((n_group * capacity, tile_edge, sketch_cols), jnp.fl...  14.6 us
  transfers between devices with their start and end apart: 10, of which 9 were waited for; matrix products, arithmetic and copies ran while one was open for 8% of the time, Pallas kernels for 0%

commit v1 on v0

v1 whole, which is shorter than its diff:
```python
import functools

import jax
import jax.numpy as jnp
from jax import lax
from jax.experimental import pallas as pl
from jax.experimental.pallas import tpu as pltpu
from jax.sharding import Mesh
from jax.sharding import PartitionSpec as P

AXES = ("z", "c", "x", "y")
MESH = pl.DeviceIdType.MESH
BF16 = jnp.bfloat16
F32 = jnp.float32
T = 128
NZ = 8
HIGH = lax.Precision.HIGHEST
NT = (((1,), (1,)), ((), ()))
ANY = pl.BlockSpec(memory_space=pl.ANY)
VMEM = pl.BlockSpec(memory_space=pltpu.VMEM)
SMEM = pl.BlockSpec(memory_space=pltpu.SMEM)
MIB = 1 << 20


def place():
    return {a: lax.axis_index(a) for a in AXES}


def moved(at, axis, step, size):
    there = dict(at)
    there[axis] = lax.rem(at[axis] + (step + size), size)
    return tuple(there[a] for a in AXES)


def greet(devices):
    barrier = pltpu.get_barrier_semaphore()
    for device in devices:
        pl.semaphore_signal(barrier, inc=1, device_id=device, device_id_type=MESH)
    pl.semaphore_wait(barrier, len(devices))


def params(mib, cid=None):
    if cid is None:
        return pltpu.CompilerParams(vmem_limit_bytes=mib * MIB)
    return pltpu.CompilerParams(
        vmem_limit_bytes=mib * MIB, collective_id=cid, has_side_effects=True
    )


def omega_kernel(omega_ref, out_ref, send, recv):
    at = place()

    def index(axis, step):
        there = moved(at, axis, step, 4)
        return there[2] * 4 + there[3]

    def index2(first, step1, second, step2):
        there = dict(at)
        there[first] = lax.rem(at[first] + (step1 + 4), 4)
        there[second] = lax.rem(at[second] + (step2 + 4), 4)
        return there["x"] * 4 + there["y"]

    me = at["x"] * 4 + at["y"]
    for b in range(4):
        out_ref[me, b] = omega_ref[b * T : (b + 1) * T, :].T
    greet([moved(at, "x", 1, 4), moved(at, "x", -1, 4), moved(at, "y", 1, 4), moved(at, "y", -1, 4)])

    def copy(i, k, axis, step, dev, lo, n):
        part = out_ref.at[dev, pl.ds(lo, n)]
        return pltpu.make_async_remote_copy(
            src_ref=part,
            dst_ref=part,
            send_sem=send.at[i, k],
            recv_sem=recv.at[i, k],
            device_id=moved(at, axis, step, 4),
            device_id_type=MESH,
        )

    sent = []

    def go(*args):
        c = copy(*args)
        c.start()
        sent.append(c)

    def begin(i, axis, dev, h):
        go(i, 0, axis, 1, dev, 2 * h, 2)
        go(i, 1, axis, -1, dev, 2 * h, 2)

    def got(i, k, axis, dev, lo, n):
        copy(i, k, axis, 1, dev, lo, n).wait_recv()

    turns = ((0, "x", "y"), (1, "y", "x"))
    for h, a, b in turns:
        begin(5 * h, a, me, h)
    for h, a, b in turns:
        begin(5 * h + 1, b, me, h)
    for h, a, b in turns:
        i = 5 * h
        got(i, 0, a, index(a, -1), 2 * h, 2)
        go(i, 2, a, 1, index(a, -1), 2 * h, 1)
        got(i, 1, a, index(a, 1), 2 * h, 2)
        go(i, 3, a, -1, index(a, 1), 2 * h + 1, 1)
    for h, a, b in turns:
        begin(5 * h + 2, b, index(a, -1), h)
        begin(5 * h + 3, b, index(a, 1), h)
    for h, a, b in turns:
        i = 5 * h
        got(i, 2, a, index(a, 2), 2 * h, 1)
        got(i, 3, a, index(a, 2), 2 * h + 1, 1)
        begin(5 * h + 4, b, index(a, 2), h)
    steps = ((1, 0), (2, -1), (3, 1), (4, 2))
    for k, d in steps:
        for h, a, b in turns:
            i = 5 * h + k
            got(i, 0, b, index2(a, d, b, -1), 2 * h, 2)
            go(i, 2, b, 1, index2(a, d, b, -1), 2 * h, 1)
            got(i, 1, b, index2(a, d, b, 1), 2 * h, 2)
            go(i, 3, b, -1, index2(a, d, b, 1), 2 * h + 1, 1)
    for k, d in steps:
        for h, a, b in turns:
            i = 5 * h + k
            got(i, 2, b, index2(a, d, b, 2), 2 * h, 1)
            got(i, 3, b, index2(a, d, b, 2), 2 * h + 1, 1)
    for c in sent:
        c.wait_send()


def gather_omega(omega):
    return pl.pallas_call(
        omega_kernel,
        out_shape=jax.ShapeDtypeStruct((16, 4, T, T), BF16),
        in_specs=[VMEM],
        out_specs=VMEM,
        scratch_shapes=[pltpu.SemaphoreType.DMA((10, 4)), pltpu.SemaphoreType.DMA((10, 4))],
        compiler_params=params(16, 1),
        name="omega_gather",
    )(omega)


STEP = 8


def sketch_kernel(col, group, slot, live, tiles_ref, omega_ref, out_ref, acc):
    step = pl.program_id(0)

    @pl.when(step == 0)
    def _():
        @pl.loop(0, 256)
        def _(i):
            acc[i] = jnp.zeros((T, T), F32)

    @pl.loop(0, STEP, unroll=4)
    def _(i):
        r = step * STEP + i
        tile_row = jnp.concatenate([tiles_ref[i, j] for j in range(5)], axis=1)
        om = jnp.concatenate([omega_ref[col[r, j]] for j in range(5)], axis=1)
        part = lax.dot_general(om, tile_row, NT, preferred_element_type=F32)
        at = group[r] * 16 + slot[r]
        acc[at] += jnp.where(r < live[0], part, 0.0)

    @pl.when(step == pl.num_programs(0) - 1)
    def _():
        @pl.loop(0, 256, unroll=2)
        def _(i):
            out_ref[i] = acc[i].astype(BF16)


def sketch_parts(tiles, tile_col, strip_group, strip_slot, live_count, omega_all):
    strips = tiles.shape[0]
    return pl.pallas_call(
        sketch_kernel,
        out_shape=jax.ShapeDtypeStruct((256, T, T), BF16),
        grid=(strips // STEP,),
        in_specs=[
            SMEM,
            SMEM,
            SMEM,
            SMEM,
            pl.BlockSpec((STEP, 5, T, T), lambda i: (i, 0, 0, 0)),
            pl.BlockSpec((64, T, T), lambda i: (0, 0, 0)),
        ],
        out_specs=pl.BlockSpec((256, T, T), lambda i: (0, 0, 0)),
        scratch_shapes=[pltpu.VMEM((256, T, T), F32)],
        compiler_params=params(52),
        name="sketch",
    )(tile_col, strip_group, strip_slot, live_count, tiles, omega_all)


ORDER = (4, 3, 5, 2, 6, 1, 7, 0)
SUB = 4


def reduce_kernel(
    x_ref, idf_ref, st_ref, wt_ref, gram_ref,
    own, sib, out_r, out_l, in_r, in_l,
    own_sem, sib_send, sib_recv, r_send, r_recv, l_send, l_recv,
):
    at = place()
    sibling = (at["z"], 1 - at["c"], at["x"], at["y"])
    greet([sibling, moved(at, "z", 1, NZ), moved(at, "z", -1, NZ)])
    mine, theirs, slot_of = [], [], {}
    for q, d in enumerate(ORDER):
        slot_of[d] = q
        z = lax.rem(at["z"] + d, NZ)
        a = pltpu.make_async_remote_copy(
            src_ref=x_ref.at[2 * z + 1 - at["c"]],
            dst_ref=sib.at[q],
            send_sem=sib_send.at[q],
            recv_sem=sib_recv.at[q],
            device_id=sibling,
            device_id_type=MESH,
        )
        b = pltpu.make_async_copy(x_ref.at[2 * z + at["c"]], own.at[q], own_sem.at[q])
        a.start()
        b.start()
        mine.append(b)
        theirs.append(a)
    ready = set()

    def need(q):
        if q not in ready:
            ready.add(q)
            mine[q].wait()
            theirs[q].wait_recv()

    sent = []

    def copy(right, s, sub):
        rows = pl.ds(sub * SUB, SUB)
        return pltpu.make_async_remote_copy(
            src_ref=(out_r if right else out_l).at[s, rows],
            dst_ref=(in_r if right else in_l).at[s, rows],
            send_sem=(r_send if right else l_send).at[s, sub],
            recv_sem=(r_recv if right else l_recv).at[s, sub],
            device_id=moved(at, "z", 1 if right else -1, NZ),
            device_id_type=MESH,
        )

    def send(right, s, sub, add):
        d = (4 - s) if right else (4 + s)
        q = slot_of[d]
        need(q)
        if add:
            copy(right, s - 1, sub).wait_recv()

        @pl.loop(sub * SUB, (sub + 1) * SUB)
        def _(b):
            v = own[q, b].astype(F32) + sib[q, b].astype(F32)
            if add:
                v = v + (in_r if right else in_l)[s - 1, b].astype(F32)
            (out_r if right else out_l)[s, b] = v.astype(BF16)

        c = copy(right, s, sub)
        c.start()
        sent.append(c)

    for sub in (0, 1):
        send(True, 0, sub, False)
        send(False, 0, sub + 2, False)
    for sub in (0, 1):
        send(True, 1, sub + 2, False)
        send(False, 1, sub, False)
    for sub in (0, 1):
        send(True, 1, sub, True)
        send(False, 1, sub + 2, True)
    for s in (2, 3):
        for sub in (2, 3, 0, 1):
            send(True, s, sub, True)
            send(False, s, (sub + 2) % 4, True)
    q = slot_of[0]
    need(q)
    gram_ref[...] = jnp.zeros((T, T), F32)
    for sub in (2, 3, 0, 1):
        copy(True, 3, sub).wait_recv()
        copy(False, 3, sub).wait_recv()

        @pl.loop(sub * SUB, (sub + 1) * SUB)
        def _(b):
            v = own[q, b].astype(F32) + sib[q, b].astype(F32)
            v = v + in_r[3, b].astype(F32) + in_l[3, b].astype(F32)
            w = idf_ref[pl.ds(b, 1), :]
            v = v * w
            st_ref[b] = v
            wt_ref[b] = (v * w).astype(BF16)
            gram_ref[...] += lax.dot_general(v, v, NT, precision=HIGH, preferred_element_type=F32)

    for c in theirs:
        c.wait_send()
    for c in sent:
        c.wait_send()


def reduce_sketch(parts, idf):
    dma = pltpu.SemaphoreType.DMA
    return pl.pallas_call(
        reduce_kernel,
        out_shape=(
            jax.ShapeDtypeStruct((16, T, T), F32),
            jax.ShapeDtypeStruct((16, T, T), BF16),
            jax.ShapeDtypeStruct((T, T), F32),
        ),
        in_specs=[ANY, VMEM],
        out_specs=(VMEM, VMEM, VMEM),
        scratch_shapes=[
            pltpu.VMEM((8, 16, T, T), BF16),
            pltpu.VMEM((8, 16, T, T), BF16),
            *[pltpu.VMEM((4, 16, T, T), BF16)] * 4,
            dma((8,)), dma((8,)), dma((8,)),
            *[dma((4, 4))] * 4,
        ],
        compiler_params=params(40, 2),
        name="sketch_reduce",
    )(parts.reshape(16, 16, T, T), idf.reshape(16, T))


def gram_kernel(
    g_ref, out_ref, half, from_sib, over_z, piece, over_xy, total, whole,
    a_send, a_recv, z_send, z_recv, p_send, p_recv, b_send, b_recv, s_send, s_recv,
):
    at = place()
    z, c, x, y = (at[a] for a in AXES)
    sibling = (z, 1 - c, x, y)
    z_peers = [moved(at, "z", d, NZ) for d in range(1, NZ)]
    xy_peers = [
        (z, c, lax.rem(x + i, 4), lax.rem(y + j, 4)) for i in range(4) for j in range(4) if i or j
    ]
    greet([sibling, *z_peers, *xy_peers])

    def put(src, dst, ss, rs, device):
        return pltpu.make_async_remote_copy(
            src_ref=src, dst_ref=dst, send_sem=ss, recv_sem=rs, device_id=device, device_id_type=MESH
        )

    def rows(i, n):
        return pl.ds(pl.multiple_of(i * n, n), n)

    one = put(g_ref.at[rows(1 - c, 64)], from_sib, a_send, a_recv, sibling)
    one.start()
    one.wait()
    half[...] = g_ref[rows(c, 64), :] + from_sib[...]
    copies = []
    for d, peer in enumerate(z_peers):
        cp = put(half.at[rows(peer[0], 8)], over_z.at[z], z_send.at[d], z_recv.at[d], peer)
        cp.start()
        copies.append(cp)
    over_z[z] = half[rows(z, 8), :]
    for cp in copies:
        cp.wait()
    piece[...] = functools.reduce(lambda u, v: u + v, [over_z[i] for i in range(NZ)])
    copies = []
    me = x * 4 + y
    for d, peer in enumerate(xy_peers):
        cp = put(piece, over_xy.at[me], p_send.at[d], p_recv.at[d], peer)
        cp.start()
        copies.append(cp)
    over_xy[me] = piece[...]
    for cp in copies:
        cp.wait()
    total[rows(z, 8), :] = functools.reduce(lambda u, v: u + v, [over_xy[i] for i in range(16)])
    copies = []
    for d, peer in enumerate(z_peers):
        cp = put(total.at[rows(z, 8)], total.at[rows(z, 8)], b_send.at[d], b_recv.at[d], peer)
        cp.start()
        copies.append(cp)
    for cp in copies:
        cp.wait()
    one = put(total, whole.at[rows(c, 64)], s_send, s_recv, sibling)
    one.start()
    whole[rows(c, 64), :] = total[...]
    one.wait()
    out_ref[...] = whole[...]


def sum_gram(gram):
    dma = pltpu.SemaphoreType.DMA
    return pl.pallas_call(
        gram_kernel,
        out_shape=jax.ShapeDtypeStruct((T, T), F32),
        in_specs=[VMEM],
        out_specs=VMEM,
        scratch_shapes=[
            pltpu.VMEM((64, T), F32),
            pltpu.VMEM((64, T), F32),
            pltpu.VMEM((8, 8, T), F32),
            pltpu.VMEM((8, T), F32),
            pltpu.VMEM((16, 8, T), F32),
            pltpu.VMEM((64, T), F32),
            pltpu.VMEM((T, T), F32),
            dma, dma, dma((7,)), dma((7,)), dma((15,)), dma((15,)), dma((7,)), dma((7,)), dma, dma,
        ],
        compiler_params=params(16, 3),
        cost_estimate=pl.CostEstimate(flops=20_000_000_000, bytes_accessed=131072, transcendentals=0),
        name="gram_sum",
    )(gram)


def basis_kernel(terms, gram_ref, st_ref, q_ref, linv_ref, work, pivots):
    work[:, :T] = gram_ref[...] * (1.0 / terms)
    row = lax.broadcasted_iota(jnp.int32, (T, T), 0)
    lane = lax.broadcasted_iota(jnp.int32, (T, T), 1)
    work[:, T:] = (row == lane).astype(F32)
    pivots[...] = jnp.zeros((T, T), F32)

    @pl.loop(0, T)
    def _(j):
        line = work[pl.ds(j, 1), :]
        pivot = jnp.sum(jnp.where(lane[:1] == j, line[:, :T], 0.0), axis=1, keepdims=True)
        scaled = line / pivot
        column = jnp.sum(jnp.where(lane == j, work[:, :T], 0.0), axis=1, keepdims=True)
        column = jnp.where(row[:, :1] > j, column, 0.0)
        work[...] = work[...] - column * scaled
        pivots[pl.ds(j, 1), :] = jnp.broadcast_to(pivot, (1, T))

    linv = work[:, T:] * lax.rsqrt(pivots[...])
    linv_ref[...] = linv

    @pl.loop(0, 16)
    def _(b):
        q_ref[pl.ds(b * T, T), :] = lax.dot_general(
            st_ref[b], linv, (((0,), (1,)), ((), ())), precision=HIGH, preferred_element_type=F32
        )


def basis(gram, st, terms):
    return pl.pallas_call(
        functools.partial(basis_kernel, terms),
        out_shape=(jax.ShapeDtypeStruct((16 * T, T), F32), jax.ShapeDtypeStruct((T, T), F32)),
        in_specs=[VMEM, VMEM],
        out_specs=(VMEM, VMEM),
        scratch_shapes=[pltpu.VMEM((T, 2 * T), F32), pltpu.VMEM((T, T), F32)],
        compiler_params=params(16),
        cost_estimate=pl.CostEstimate(flops=20_000_000_000, bytes_accessed=2 * MIB, transcendentals=0),
        name="basis",
    )(gram, st)


def project_kernel(col, group, slot, live, tiles_ref, w_ref, acc):
    step = pl.program_id(0)

    @pl.when(step == 0)
    def _():
        @pl.loop(0, 64)
        def _(i):
            acc[i] = jnp.zeros((T, T), F32)

    @pl.loop(0, STEP, unroll=2)
    def _(i):
        r = step * STEP + i
        tile_row = jnp.concatenate([tiles_ref[i, j] for j in range(5)], axis=1)
        w = w_ref[group[r] * 16 + slot[r]]
        w = jnp.where(r < live[0], w, jnp.zeros_like(w))
        part = jnp.dot(w, tile_row, preferred_element_type=F32)
        for j in range(5):
            c = col[r, j]
            dev, b = c // 4, c % 4
            flow = b // 2
            u, v = dev // 4, dev % 4
            t = jnp.where(flow == 0, u * 4 + v, v * 4 + u)
            acc[flow * 32 + t * 2 + b % 2] += part[:, j * T : (j + 1) * T]


def project(tiles, tile_col, strip_group, strip_slot, live_count, weighted):
    strips = tiles.shape[0]
    return pl.pallas_call(
        project_kernel,
        out_shape=jax.ShapeDtypeStruct((64, T, T), F32),
        grid=(strips // STEP,),
        in_specs=[
            SMEM,
            SMEM,
            SMEM,
            SMEM,
            pl.BlockSpec((STEP, 5, T, T), lambda i: (i, 0, 0, 0)),
            pl.BlockSpec((256, T, T), lambda i: (0, 0, 0)),
        ],
        out_specs=pl.BlockSpec((64, T, T), lambda i: (0, 0, 0)),
        compiler_params=params(48),
        name="project",
    )(tile_col, strip_group, strip_slot, live_count, tiles, weighted)


def ring_sum(at, axis, own, out_refs, in_refs, send, recv, size):
    here = at[axis]
    dtype = out_refs[0].dtype
    low, high = pl.ds(0, size), pl.ds(size, size)
    r0, r1, l0, l1 = range(4)
    sent = []

    def copy(k, src, dst, right):
        return pltpu.make_async_remote_copy(
            src_ref=src,
            dst_ref=dst,
            send_sem=send.at[k],
            recv_sem=recv.at[k],
            device_id=moved(at, axis, 1 if right else -1, 4),
            device_id_type=MESH,
        )

    def fill(k, offset, target, extra=None):
        out = out_refs[k]
        base = 0 if k in (r0, l0) else offset

        @pl.loop(0, size)
        def _(b):
            v = own[target, b + offset]
            if extra is not None:
                v = v + extra[b].astype(F32)
            out[base + b] = v.astype(dtype)

    far = lax.rem(here + 2, 4)
    right, left = lax.rem(here + 1, 4), lax.rem(here + 3, 4)
    c_r0 = copy(0, out_refs[r0], in_refs[r0], True)
    c_l0 = copy(1, out_refs[l0], in_refs[l0], False)
    c_r1q = copy(2, out_refs[r1].at[high], in_refs[r1].at[high], True)
    c_l1p = copy(3, out_refs[l1].at[low], in_refs[l1].at[low], False)
    c_r1p = copy(4, out_refs[r1].at[low], in_refs[r1].at[low], True)
    c_l1q = copy(5, out_refs[l1].at[high], in_refs[l1].at[high], False)
    fill(r0, 0, far)
    c_r0.start()
    fill(l0, size, far)
    c_l0.start()
    yield
    fill(r1, size, right)
    c_r1q.start()
    fill(l1, 0, left)
    c_l1p.start()
    yield
    c_r0.wait_recv()
    fill(r1, 0, right, in_refs[r0])
    c_r1p.start()
    c_l0.wait_recv()
    fill(l1, size, left, in_refs[l0])
    c_l1q.start()
    yield
    for c in (c_r1q, c_l1p, c_r1p, c_l1q):
        c.wait_recv()
    yield
    for c in (c_r0, c_l0, c_r1q, c_l1p, c_r1p, c_l1q):
        c.wait_send()
    yield


def docs_kernel(part_ref, linv_ref, out_ref, *scratch):
    at = place()
    bufs1 = [scratch[0:8], scratch[8:16]]
    bufs2 = [scratch[16:24], scratch[24:32]]
    sums, final, send, recv = scratch[32:]
    greet([moved(at, "x", 1, 4), moved(at, "x", -1, 4), moved(at, "y", 1, 4), moved(at, "y", -1, 4)])
    axes = ("x", "y")
    runs = [
        ring_sum(
            at, axes[f], part_ref.at[f], bufs1[f][:4], bufs1[f][4:], send.at[f], recv.at[f], 4
        )
        for f in range(2)
    ]
    for _ in range(4):
        for run in runs:
            next(run)
    for f in range(2):
        in_r, in_l = bufs1[f][5], bufs1[f][7]
        here = at[axes[f]]

        @pl.loop(0, 8)
        def _(b):
            v = part_ref[f, here, b] + in_r[b].astype(F32) + in_l[b].astype(F32)
            sums[f, b // 2, b % 2] = v

    later = [
        ring_sum(
            at, axes[1 - f], sums.at[f], bufs2[f][:4], bufs2[f][4:], send.at[2 + f], recv.at[2 + f], 1
        )
        for f in range(2)
    ]
    for _ in range(4):
        for run in later:
            next(run)
    for f in range(2):
        in_r, in_l = bufs2[f][5], bufs2[f][7]
        here = at[axes[1 - f]]
        for b in range(2):
            final[2 * f + b] = sums[f, here, b] + in_r[b] + in_l[b]
    for b in range(4):
        out_ref[:, b * T : (b + 1) * T] = jnp.dot(
            linv_ref[...], final[b], precision=HIGH, preferred_element_type=F32
        ).astype(BF16)
    for run in (*runs, *later):
        next(run)


def sum_docs(parts, linv):
    dma = pltpu.SemaphoreType.DMA

    def bufs(size, dtype):
        return [pltpu.VMEM((n * size, T, T), dtype) for n in (1, 2, 1, 2)] * 2

    return pl.pallas_call(
        docs_kernel,
        out_shape=jax.ShapeDtypeStruct((T, 4 * T), BF16),
        in_specs=[VMEM, VMEM],
        out_specs=VMEM,
        scratch_shapes=[
            *bufs(4, BF16),
            *bufs(4, BF16),
            *bufs(1, F32),
            *bufs(1, F32),
            pltpu.VMEM((2, 4, 2, T, T), F32),
            pltpu.VMEM((4, T, T), F32),
            dma((4, 6)),
            dma((4, 6)),
        ],
        compiler_params=params(24, 4),
        name="docs_sum",
    )(parts.reshape(2, 4, 8, T, T), linv)


def on_device(tiles, tile_col, strip_group, strip_slot, live_count, omega, idf):
    terms = idf.shape[0] * 256
    omega_all = gather_omega(omega).reshape(64, T, T)
    where = (tile_col, strip_group, strip_slot, live_count)
    parts = sketch_parts(tiles, *where, omega_all)
    st, wt, gram = reduce_sketch(parts, idf)
    weighted = lax.all_gather(wt, ("z", "c"), axis=0, tiled=True)
    gram = sum_gram(gram)
    q_basis, linv = basis(gram, st, terms)
    doc_parts = project(tiles, *where, weighted)
    doc_factor = sum_docs(doc_parts, linv)
    return q_basis, doc_factor


def solution(mesh):
    torus = Mesh(mesh.devices.reshape(8, 2, 4, 4), AXES)
    in_specs = (
        P(AXES, None, None, None),
        P(AXES, None),
        P(AXES),
        P(AXES),
        P(AXES),
        P(AXES, None),
        P(AXES),
    )
    out_specs = (P(AXES, None), P(None, AXES))
    return jax.shard_map(
        on_device, mesh=torus, in_specs=in_specs, out_specs=out_specs, check_vma=False
    )
```

time: 601 us -> 208 us (0.35)
  waiting for transfers between devices: 336 us -> 14.9 us
  Pallas kernels: 0 us -> 169 us
  other arithmetic: 105 us -> 0 us
  starting transfers between devices: 48.8 us -> 0.04 us
  local copies, waits for them, and re-layouts: 54.9 us -> 8.4 us
  matrix products: 39.3 us -> 0 us
    all_to_all x8 -> x0, waiting for transfers between devices: 262 us -> none  [the longest x1 139 us: on_device(): lax.all_to_all(outgoing.reshape(n_group, capacity, tile_edge, sketch_cols...]
    pallas_call x0 -> x7, Pallas kernels: none -> 169 us  [the longest x1 51.1 us: reduce_sketch(): pl.pallas_call(reduce_kernel, out_shape=(jax.ShapeDtypeStruct((16, T, T),...]
    scatter-add x1 -> x0, other arithmetic: 74.8 us -> none  [on_device(): jax.ops.segment_sum(contrib.reshape(-1, sketch_cols, tile_edge), tile_col...]
    reduce_scatter x2 -> x0, waiting for transfers between devices: 74.5 us -> none  [summed_rows_2(): nearer = lax.psum_scatter(value, axes[0], scatter_dimension=dim, tiled=True)]
    all_to_all x8 -> x0, starting transfers between devices: 48.4 us -> none  [the longest x3 16.5 us: sent_to_all(): lax.all_to_all(jnp.broadcast_to(value[None], (count, *value.shape)), axis...]
    dot_general x4 -> x0, matrix products: 37.4 us -> none  [the longest x1 15.5 us: on_device(): jnp.einsum('sik,stij->stkj', strip_q, tiles, preferred_element_type=jnp.f...]
    another operation x6 -> x0, other arithmetic: 23 us -> none  [the longest x3 12.4 us: on_device(): lower_factor = jnp.linalg.cholesky(gram_matrix)]
    gather x3 -> x0, local copies, waits for them, and re-layouts: 16.8 us -> none  [the longest x1 11.1 us: on_device(): picked = omega_blocks[tile_col]]
  transfers between devices with their start and end apart: 10 -> 1, of which waited for: 9 -> 1; matrix products, arithmetic and copies ran while one was open for 8% -> 0% of each run, Pallas kernels for 0% -> 19%
where the time goes in v1:
time: 208 us; the launch traced here: 207 us
  Pallas kernels  169 us (81%)
  waiting for transfers between devices  14.9 us (7%)
  between operations  14.7 us (7%)
  local copies, waits for them, and re-layouts  8.4 us (4%)
    pallas_call x1, Pallas kernels, reduce_sketch(): pl.pallas_call(reduce_kernel, out_shape=(jax.ShapeDtypeStruct((16, T, T),...  51.1 us
    pallas_call x1, Pallas kernels, sum_docs(): pl.pallas_call(docs_kernel, out_shape=jax.ShapeDtypeStruct((T, 4 * T), BF...  23.2 us
    pallas_call x1, Pallas kernels, sum_gram(): pl.pallas_call(gram_kernel, out_shape=jax.ShapeDtypeStruct((T, T), F32),...  21.7 us
    pallas_call x1, Pallas kernels, gather_omega(): pl.pallas_call(omega_kernel, out_shape=jax.ShapeDtypeStruct((16, 4, T, T)...  19.3 us
    pallas_call x1, Pallas kernels, basis(): pl.pallas_call(functools.partial(basis_kernel, terms), out_shape=(jax.Sha...  18.6 us
    pallas_call x1, Pallas kernels, project(): pl.pallas_call(project_kernel, out_shape=jax.ShapeDtypeStruct((64, T, T),...  18.1 us
    pallas_call x1, Pallas kernels, sketch_parts(): pl.pallas_call(sketch_kernel, out_shape=jax.ShapeDtypeStruct((256, T, T),...  17 us
    all_gather x1, waiting for transfers between devices, on_device(): weighted = lax.all_gather(wt, ('z', 'c'), axis=0, tiled=True)  14.9 us
  transfers between devices with their start and end apart: 1, of which 1 were waited for; matrix products, arithmetic and copies ran while one was open for 0% of the time, Pallas kernels for 19%

profile of v1, /device:TPU:2, one launch (start us, length us, event | category | flops | bytes accessed | tf_op | source)
XLA Modules:
  0.0 207.2 jit_solution(2335826891010066721)
XLA Ops:
  7.2 0.0 all-gather.2.cloned.1.call-start
  7.9 0.8 copy.11.col
  8.6 0.0 copy-start.2
  8.6 0.9 copy-done.2
  9.5 19.3 %omega_gather.1 = bf16[16,4,128,128]{3,2,1,0:T(8,128)(2,1)S(1)} custom-call(bf16[512,128]{1,0:T(8,128)(2,1)S(1)} %copy-done.2), custom_call_target="tpu_custom_call" | custom-call | tf_op jit(solution)/shard_map/omega_gather/pallas_call | solution.py:130
  28.9 0.0 copy-start.1
  28.9 1.4 copy-done.1
  30.2 0.0 copy-start.4
  30.2 0.7 copy-done.4
  30.9 0.0 copy-start.6
  30.9 0.7 copy-done.6
  31.5 0.0 copy-start.3
  31.5 17.0 %sketch.1 = bf16[256,128,128]{2,1,0:T(8,128)(2,1)} custom-call(s32[72,5]{1,0:T(8,128)S(1)} %copy.11.col, s32[72]{0:T(128)S(1)} %copy-done.4, s32[72]{0:T(128)S(1)} %copy-done.6, s32[1]{0:T(128)S(6)} %copy.14.live, bf16[72,5,128,128]{3,2,1,0:T(8,128)(2,1)} %tiles_ref.3, bf16[64,128,128]{2,1,0:T(8,128)(2,1)} %bitcast.6), custom_call_target="tpu_custom_call" | custom-call | tf_op jit(solution)/shard_map/sketch/pallas_call | solution.py:171
  48.6 0.0 copy-done.3
  48.6 0.0 copy-start
  48.6 3.4 %copy-done = bf16[256,128,128]{2,1,0:T(8,128)(2,1)S(1)} copy-done((bf16[256,128,128]{2,1,0:T(8,128)(2,1)S(1)}, bf16[256,128,128]{2,1,0:T(8,128)(2,1)}, u32[]{:S(2)}) %copy-start) | copy-done | bytes 8388632
  52.0 51.1 %sketch_reduce.1 = (f32[16,128,128]{2,1,0:T(8,128)S(1)}, bf16[16,128,128]{2,1,0:T(8,128)(2,1)}, f32[128,128]{1,0:T(8,128)S(1)}) custom-call(bf16[16,16,128,128]{3,2,1,0:T(8,128)(2,1)S(1)} %bitcast.4, f32[16,128]{1,0:T(8,128)S(1)} %bitcast.7), custom_call_target="tpu_custom_call" | custom-call | tf_op jit(solution)/shard_map/sketch_reduce/pallas_call | solution.py:296
  103.1 0.0 all-gather.2.cloned.1.call-update
  103.1 21.7 %gram_sum.1.gram_ref = f32[128,128]{1,0:T(8,128)S(1)} custom-call(f32[128,128]{1,0:T(8,128)S(1)} %get-tuple-element.7.g_ref), custom_call_target="tpu_custom_call" | custom-call | flops 20000000000 | bytes 131072 | tf_op jit(solution)/shard_map/gram_sum/pallas_call | solution.py:377
  124.8 0.0 copy-start.5
  124.8 0.0 copy-start.7
  124.9 18.6 %basis.1 = (f32[2048,128]{1,0:T(8,128)}, f32[128,128]{1,0:T(8,128)S(1)}) custom-call(f32[128,128]{1,0:T(8,128)S(1)} %gram_sum.1.gram_ref, f32[16,128,128]{2,1,0:T(8,128)S(1)} %get-tuple-element.8.st_ref), custom_call_target="tpu_custom_call" | custom-call | flops 20000000000 | bytes 2097152 | tf_op jit(solution)/shard_map/basis/pallas_call | solution.py:426
  143.5 14.9 %all-gather.2.cloned.1.call-done.w_ref = bf16[256,128,128]{2,1,0:T(8,128)(2,1)} async-done(((bf16[16,128,128]{2,1,0:T(8,128)(2,1)}), bf16[256,128,128]{2,1,0:T(8,128)(2,1)}) %all-gather.2.cloned.1.call-update) | async-done | bytes 8388624 | tf_op jit(solution)/shard_map/all_gather | solution.py:623
  158.3 0.0 copy-done.5
  158.3 0.0 copy-done.7
  158.3 18.1 %project.1 = f32[64,128,128]{2,1,0:T(8,128)S(1)} custom-call(s32[72,5]{1,0:T(8,128)S(1)} %copy.11.col, s32[72]{0:T(128)S(1)} %copy-done.5, s32[72]{0:T(128)S(1)} %copy-done.7, s32[1]{0:T(128)S(6)} %copy.14.live, bf16[72,5,128,128]{3,2,1,0:T(8,128)(2,1)} %tiles_ref.3, bf16[256,128,128]{2,1,0:T(8,128)(2,1)} %all-gather.2.cloned.1.call-done.w_ref), custom_call_target="tpu_custom_call" | custom-call | tf_op jit(solution)/shard_map/project/pallas_call | solution.py:465
  176.5 23.2 %docs_sum.1 = bf16[128,512]{1,0:T(8,128)(2,1)S(1)} custom-call(f32[2,4,8,128,128]{4,3,2,1,0:T(8,128)S(1)} %bitcast.5, f32[128,128]{1,0:T(8,128)S(1)} %get-tuple-element.11.linv_ref), custom_call_target="tpu_custom_call" | custom-call | tf_op jit(solution)/shard_map/docs_sum/pallas_call | solution.py:597
  199.7 0.7 copy.15
Async XLA Ops:
  7.2 151.2 %all-gather.2.cloned.1.call-start = ((), (), s32[]{:S(2)}) async-start(), calls=%async_computation | async-start | bytes 8912896 | tf_op jit(solution)/shard_map/all_gather | solution.py:623
  8.6 0.9 copy-start.2
  28.9 1.4 copy-start.1
  30.2 0.7 copy-start.4
  30.9 0.7 copy-start.6
  31.5 17.1 %copy-start.3 = (f32[2048]{0:T(1024)S(1)}, f32[2048]{0:T(1024)}, u32[]{:S(2)}) copy-start(f32[2048]{0:T(1024)} %param.13) | copy-start | bytes 24580
  48.6 3.4 %copy-start = (bf16[256,128,128]{2,1,0:T(8,128)(2,1)S(1)}, bf16[256,128,128]{2,1,0:T(8,128)(2,1)}, u32[]{:S(2)}) copy-start(bf16[256,128,128]{2,1,0:T(8,128)(2,1)} %sketch.1) | copy-start | bytes 25165828
  124.8 33.5 %copy-start.5 = (s32[72]{0:T(128)S(1)}, s32[72]{0:T(128)}, u32[]{:S(2)}) copy-start(s32[72]{0:T(128)} %group.3) | copy-start | bytes 868
  124.8 33.5 %copy-start.7 = (s32[72]{0:T(128)S(1)}, s32[72]{0:T(128)}, u32[]{:S(2)}) copy-start(s32[72]{0:T(128)} %slot.3) | copy-start | bytes 868
Sparse Core Ops, SparseCore 0:
  103.2 55.0 all-gather.1

commit v2 on v1

v2 whole, which is shorter than its diff:
```python
import functools

import jax
import jax.numpy as jnp
from jax import lax
from jax.experimental import pallas as pl
from jax.experimental.pallas import tpu as pltpu
from jax.sharding import Mesh
from jax.sharding import PartitionSpec as P

AXES = ("z", "c", "x", "y")
MESH = pl.DeviceIdType.MESH
BF16 = jnp.bfloat16
F32 = jnp.float32
T = 128
NZ = 8
HIGH = lax.Precision.HIGHEST
NT = (((1,), (1,)), ((), ()))
ANY = pl.BlockSpec(memory_space=pl.ANY)
VMEM = pl.BlockSpec(memory_space=pltpu.VMEM)
SMEM = pl.BlockSpec(memory_space=pltpu.SMEM)
MIB = 1 << 20


def place():
    return {a: lax.axis_index(a) for a in AXES}


def moved(at, axis, step, size):
    there = dict(at)
    there[axis] = lax.rem(at[axis] + (step + size), size)
    return tuple(there[a] for a in AXES)


def greet(devices):
    barrier = pltpu.get_barrier_semaphore()
    for device in devices:
        pl.semaphore_signal(barrier, inc=1, device_id=device, device_id_type=MESH)
    pl.semaphore_wait(barrier, len(devices))


def params(mib, cid=None):
    if cid is None:
        return pltpu.CompilerParams(vmem_limit_bytes=mib * MIB)
    return pltpu.CompilerParams(
        vmem_limit_bytes=mib * MIB, collective_id=cid, has_side_effects=True
    )


STEP = 8
PER = 6
NONE = 6


def lists_kernel(group, slot, live, strip, before, last, count):
    @pl.loop(0, 16)
    def _(o):
        count[o] = 0

    @pl.loop(0, 256, unroll=8)
    def _(k):
        last[k] = NONE

    @pl.loop(0, 16 * PER, unroll=8)
    def _(k):
        strip[k] = 0
        before[k] = NONE

    @pl.loop(0, live[0])
    def _(r):
        o = group[r]
        n = count[o]
        at = o * 16 + slot[r]
        strip[o * PER + n] = r
        before[o * PER + n] = last[at]
        last[at] = n
        count[o] = n + 1


def strip_lists(strip_group, strip_slot, live_count):
    ints = jnp.int32
    return pl.pallas_call(
        lists_kernel,
        out_shape=(
            jax.ShapeDtypeStruct((16 * PER,), ints),
            jax.ShapeDtypeStruct((16 * PER,), ints),
            jax.ShapeDtypeStruct((256,), ints),
        ),
        in_specs=[SMEM, SMEM, SMEM],
        out_specs=(SMEM, SMEM, SMEM),
        scratch_shapes=[pltpu.SMEM((16,), ints)],
        name="strip_lists",
    )(strip_group, strip_slot, live_count)


ORDER = (4, 3, 5, 2, 6, 1, 7, 0)
SUB = 4
SUBW = 2
NW = 8


def gather_omega(at, omega_ref, om, send, recv):
    def index(axis, step):
        there = moved(at, axis, step, 4)
        return there[2] * 4 + there[3]

    def index2(first, step1, second, step2):
        there = dict(at)
        there[first] = lax.rem(at[first] + (step1 + 4), 4)
        there[second] = lax.rem(at[second] + (step2 + 4), 4)
        return there["x"] * 4 + there["y"]

    me = at["x"] * 4 + at["y"]

    def copy(i, k, axis, step, dev, lo, n):
        part = om.at[pl.ds(dev * 4 + lo, n)]
        return pltpu.make_async_remote_copy(
            src_ref=part,
            dst_ref=part,
            send_sem=send.at[i, k],
            recv_sem=recv.at[i, k],
            device_id=moved(at, axis, step, 4),
            device_id_type=MESH,
        )

    sent = []

    def go(*args):
        c = copy(*args)
        c.start()
        sent.append(c)

    def begin(i, axis, dev, h):
        go(i, 0, axis, 1, dev, 2 * h, 2)
        go(i, 1, axis, -1, dev, 2 * h, 2)

    def got(i, k, axis, dev, lo, n):
        copy(i, k, axis, 1, dev, lo, n).wait_recv()

    turns = ((0, "x", "y"), (1, "y", "x"))
    for h, a, b in turns:
        begin(5 * h, a, me, h)
    for h, a, b in turns:
        begin(5 * h + 1, b, me, h)
    for h, a, b in turns:
        i = 5 * h
        got(i, 0, a, index(a, -1), 2 * h, 2)
        go(i, 2, a, 1, index(a, -1), 2 * h, 1)
        begin(5 * h + 2, b, index(a, -1), h)
        got(i, 1, a, index(a, 1), 2 * h, 2)
        go(i, 3, a, -1, index(a, 1), 2 * h + 1, 1)
        begin(5 * h + 3, b, index(a, 1), h)
    for h, a, b in turns:
        i = 5 * h
        got(i, 2, a, index(a, 2), 2 * h, 1)
        got(i, 3, a, index(a, 2), 2 * h + 1, 1)
        begin(5 * h + 4, b, index(a, 2), h)
    steps = ((1, 0), (2, -1), (3, 1), (4, 2))
    for k, d in steps:
        for h, a, b in turns:
            i = 5 * h + k
            got(i, 0, b, index2(a, d, b, -1), 2 * h, 2)
            go(i, 2, b, 1, index2(a, d, b, -1), 2 * h, 1)
            got(i, 1, b, index2(a, d, b, 1), 2 * h, 2)
            go(i, 3, b, -1, index2(a, d, b, 1), 2 * h + 1, 1)
    for k, d in steps:
        for h, a, b in turns:
            i = 5 * h + k
            got(i, 2, b, index2(a, d, b, 2), 2 * h, 1)
            got(i, 3, b, index2(a, d, b, 2), 2 * h + 1, 1)
    return sent


def gram_steps(at, g_ref, whole, half, from_sib, over_z, piece, over_xy, total, sems):
    z, c, x, y = (at[a] for a in AXES)
    sibling = (z, 1 - c, x, y)
    a_send, a_recv, z_send, z_recv, p_send, p_recv, b_send, b_recv, s_send, s_recv = sems

    def put(src, dst, ss, rs, device):
        cp = pltpu.make_async_remote_copy(
            src_ref=src, dst_ref=dst, send_sem=ss, recv_sem=rs, device_id=device, device_id_type=MESH
        )
        cp.start()
        return cp

    def rows(i, n):
        return pl.ds(pl.multiple_of(i * n, n), n)

    one = put(g_ref.at[rows(1 - c, 64)], from_sib, a_send, a_recv, sibling)
    yield
    one.wait()
    half[...] = g_ref[rows(c, 64), :] + from_sib[...]
    z_peers = [moved(at, "z", d, NZ) for d in range(1, NZ)]
    copies = [
        put(half.at[rows(p[0], 8)], over_z.at[z], z_send.at[d], z_recv.at[d], p)
        for d, p in enumerate(z_peers)
    ]
    over_z[z] = half[rows(z, 8), :]
    yield
    for cp in copies:
        cp.wait()
    piece[...] = functools.reduce(lambda u, v: u + v, [over_z[i] for i in range(NZ)])
    me = x * 4 + y
    copies = [
        put(piece, over_xy.at[me], p_send.at[d], p_recv.at[d], p) for d, p in enumerate(xy_others(at))
    ]
    over_xy[me] = piece[...]
    yield
    for cp in copies:
        cp.wait()
    total[rows(z, 8), :] = functools.reduce(lambda u, v: u + v, [over_xy[i] for i in range(16)])
    copies = [
        put(total.at[rows(z, 8)], total.at[rows(z, 8)], b_send.at[d], b_recv.at[d], p)
        for d, p in enumerate(z_peers)
    ]
    yield
    for cp in copies:
        cp.wait()
    one = put(total, whole.at[rows(c, 64)], s_send, s_recv, sibling)
    whole[rows(c, 64), :] = total[...]
    yield
    one.wait()
    yield


def xy_others(at):
    z, c, x, y = (at[a] for a in AXES)
    return [(z, c, lax.rem(x + i, 4), lax.rem(y + j, 4)) for i in range(4) for j in range(4) if i or j]


def eliminate(terms, gram, linv_ref, work, pivots):
    work[:, :T] = gram[...] * (1.0 / terms)
    row = lax.broadcasted_iota(jnp.int32, (T, T), 0)
    lane = lax.broadcasted_iota(jnp.int32, (T, T), 1)
    work[:, T:] = (row == lane).astype(F32)
    pivots[...] = jnp.zeros((T, T), F32)
    for first in range(0, T, 16):

        @pl.loop(first, first + 16)
        def _(j):
            line = work[pl.ds(j, 1), :]
            pivot = jnp.sum(jnp.where(lane[:1] == j, line[:, :T], 0.0), axis=1, keepdims=True)
            scaled = line / pivot
            column = jnp.sum(jnp.where(lane == j, work[:, :T], 0.0), axis=1, keepdims=True)
            column = jnp.where(row[:, :1] > j, column, 0.0)
            work[...] = work[...] - column * scaled
            pivots[pl.ds(j, 1), :] = jnp.broadcast_to(pivot, (1, T))

        yield
    linv_ref[...] = work[:, T:] * lax.rsqrt(pivots[...])
    yield


def front_kernel(
    terms, strip, before, last, col, omega_ref, idf_ref, tiles_ref, w_ref, st_ref, linv_ref,
    tiles, om, raw, chain, own, out_sib, sib, out_r, out_l, in_r, in_l, wt, gram,
    whole, half, from_sib, over_z, piece, over_xy, total, work, pivots,
    load_sem, om_send, om_recv, sib_send, sib_recv, r_send, r_recv, l_send, l_recv,
    own_sem, wr_send, wr_recv, wl_send, wl_recv, ws_send, ws_recv, *gram_sems,
):
    at = place()
    load = pltpu.make_async_copy(tiles_ref, tiles, load_sem)
    load.start()
    sibling = (at["z"], 1 - at["c"], at["x"], at["y"])
    me = at["x"] * 4 + at["y"]
    for b in range(4):
        om[me * 4 + b] = omega_ref[b * T : (b + 1) * T, :].T
    greet([sibling, *[moved(at, "z", d, NZ) for d in range(1, NZ)], *xy_others(at)])
    sent = gather_omega(at, omega_ref, om, om_send, om_recv)

    @pl.loop(0, 2 * (PER + 1))
    def _(k):
        chain[k] = jnp.zeros((T, T), F32)

    load.wait()
    slot_of = {d: q for q, d in enumerate(ORDER)}

    def sketch(d):
        q = slot_of[d]
        z = lax.rem(at["z"] + d, NZ)
        for k, target in ((0, out_sib), (1, own)):
            o = 2 * z + (1 - at["c"] if k == 0 else at["c"])
            base = k * (PER + 1)

            @pl.loop(0, PER, unroll=3)
            def _(n):
                i = strip[o * PER + n]
                tile_row = jnp.concatenate([tiles[i, j] for j in range(5)], axis=1)
                m = jnp.concatenate([om[col[i, j]] for j in range(5)], axis=1)
                raw[k * PER + n] = lax.dot_general(m, tile_row, NT, preferred_element_type=F32)

            @pl.loop(0, PER)
            def _(n):
                chain[base + n] = raw[k * PER + n] + chain[base + before[o * PER + n]]

            @pl.loop(0, 16, unroll=2)
            def _(b):
                target[q, b] = chain[base + last[o * 16 + b]].astype(BF16)

            if k == 0:
                c = pltpu.make_async_remote_copy(
                    src_ref=out_sib.at[q],
                    dst_ref=sib.at[q],
                    send_sem=sib_send.at[q],
                    recv_sem=sib_recv.at[q],
                    device_id=sibling,
                    device_id_type=MESH,
                )
                c.start()
        sent.append(c)
        theirs[q] = c

    theirs = {}
    ready = set()

    def need(q):
        if q not in ready:
            ready.add(q)
            theirs[q].wait_recv()

    def copy(right, s, sub):
        rows = pl.ds(sub * SUB, SUB)
        return pltpu.make_async_remote_copy(
            src_ref=(out_r if right else out_l).at[s, rows],
            dst_ref=(in_r if right else in_l).at[s, rows],
            send_sem=(r_send if right else l_send).at[s, sub],
            recv_sem=(r_recv if right else l_recv).at[s, sub],
            device_id=moved(at, "z", 1 if right else -1, NZ),
            device_id_type=MESH,
        )

    def send(right, s, sub, add):
        d = (4 - s) if right else (4 + s)
        q = slot_of[d]
        need(q)
        if add:
            copy(right, s - 1, sub).wait_recv()

        @pl.loop(sub * SUB, (sub + 1) * SUB)
        def _(b):
            v = own[q, b].astype(F32) + sib[q, b].astype(F32)
            if add:
                v = v + (in_r if right else in_l)[s - 1, b].astype(F32)
            (out_r if right else out_l)[s, b] = v.astype(BF16)

        c = copy(right, s, sub)
        c.start()
        sent.append(c)

    sketch(4)
    for sub in (0, 1):
        send(True, 0, sub, False)
        send(False, 0, sub + 2, False)
    sketch(3)
    sketch(5)
    for sub in (0, 1):
        send(True, 1, sub + 2, False)
        send(False, 1, sub, False)
    for sub in (0, 1):
        send(True, 1, sub, True)
        send(False, 1, sub + 2, True)
    sketch(2)
    sketch(6)
    for s in (2, 3):
        for sub in (2, 3, 0, 1):
            send(True, s, sub, True)
            send(False, s, (sub + 2) % 4, True)
        if s == 2:
            sketch(1)
            sketch(7)
    sketch(0)

    mine = 2 * at["z"] + at["c"]

    def wcopy(right, hop, sub):
        owner = 2 * lax.rem(at["z"] + ((1 - hop) if right else (hop - 1)) + NZ, NZ) + at["c"]
        rows = pl.ds(sub * SUBW, SUBW)
        return pltpu.make_async_remote_copy(
            src_ref=wt.at[rows] if hop == 1 else w_ref.at[owner, rows],
            dst_ref=w_ref.at[owner, rows],
            send_sem=(wr_send if right else wl_send).at[hop - 1, sub],
            recv_sem=(wr_recv if right else wl_recv).at[hop - 1, sub],
            device_id=moved(at, "z", 1 if right else -1, NZ),
            device_id_type=MESH,
        )

    def wgo(right, hop, sub):
        c = wcopy(right, hop, sub)
        c.start()
        sent.append(c)

    def to_sibling(d):
        owner = 2 * lax.rem(at["z"] + d, NZ) + at["c"]
        c = pltpu.make_async_remote_copy(
            src_ref=wt if d == 0 else w_ref.at[owner],
            dst_ref=w_ref.at[owner],
            send_sem=ws_send.at[d],
            recv_sem=ws_recv.at[d],
            device_id=sibling,
            device_id_type=MESH,
        )
        c.start()
        passed.append(c)

    passed = []
    q = slot_of[0]
    need(q)
    gram[...] = jnp.zeros((T, T), F32)
    for sub in (2, 3, 0, 1):
        copy(True, 3, sub).wait_recv()
        copy(False, 3, sub).wait_recv()

        @pl.loop(sub * SUB, (sub + 1) * SUB)
        def _(b):
            v = own[q, b].astype(F32) + sib[q, b].astype(F32)
            v = v + in_r[3, b].astype(F32) + in_l[3, b].astype(F32)
            w = idf_ref[pl.ds(b, 1), :]
            v = v * w
            st_ref[b] = v
            wt[b] = (v * w).astype(BF16)

        for k in range(SUB // SUBW):
            wgo(True, 1, sub * (SUB // SUBW) + k)
            wgo(False, 1, sub * (SUB // SUBW) + k)
    to_sibling(0)
    keep = pltpu.make_async_copy(wt, w_ref.at[mine], own_sem)
    keep.start()

    @pl.loop(0, 16)
    def _(b):
        v = st_ref[b]
        gram[...] += lax.dot_general(v, v, NT, precision=HIGH, preferred_element_type=F32)

    def side():
        yield from gram_steps(
            at, gram, whole, half, from_sib, over_z, piece, over_xy, total, gram_sems
        )
        yield from eliminate(terms, whole, linv_ref, work, pivots)

    aside = side()
    next(aside)
    order = (4, 5, 6, 7, 0, 1, 2, 3)
    for hop in (2, 3, 4):
        for n, sub in enumerate(order):
            wcopy(True, hop - 1, sub).wait_recv()
            if hop < 4 or sub < NW // 2:
                wgo(True, hop, sub)
            wcopy(False, hop - 1, sub).wait_recv()
            if hop < 4 or sub >= NW // 2:
                wgo(False, hop, sub)
            if n % 2 == 1:
                next(aside, None)
        to_sibling(hop - 1)
        to_sibling(NZ - (hop - 1))
    for _ in aside:
        pass
    for sub in range(NW // 2):
        wcopy(True, 4, sub).wait_recv()
        wcopy(False, 4, sub + NW // 2).wait_recv()
    to_sibling(4)
    keep.wait()
    for c in passed:
        c.wait()
    for c in sent:
        c.wait_send()


def front(lists, tile_col, tiles, omega, idf, terms):
    dma = pltpu.SemaphoreType.DMA
    v = pltpu.VMEM
    return pl.pallas_call(
        functools.partial(front_kernel, terms),
        out_shape=(
            jax.ShapeDtypeStruct((16, 16, T, T), BF16),
            jax.ShapeDtypeStruct((16, T, T), F32),
            jax.ShapeDtypeStruct((T, T), F32),
        ),
        in_specs=[SMEM, SMEM, SMEM, SMEM, VMEM, VMEM, ANY],
        out_specs=(ANY, VMEM, VMEM),
        scratch_shapes=[
            v(tiles.shape, BF16),
            v((64, T, T), BF16),
            v((2 * PER, T, T), F32),
            v((2 * (PER + 1), T, T), F32),
            *[v((8, 16, T, T), BF16)] * 3,
            *[v((4, 16, T, T), BF16)] * 4,
            v((16, T, T), BF16),
            v((T, T), F32),
            v((T, T), F32),
            v((64, T), F32),
            v((64, T), F32),
            v((8, 8, T), F32),
            v((8, T), F32),
            v((16, 8, T), F32),
            v((64, T), F32),
            v((T, 2 * T), F32),
            v((T, T), F32),
            dma,
            dma((10, 4)), dma((10, 4)),
            dma((8,)), dma((8,)),
            *[dma((4, 4))] * 4,
            dma,
            *[dma((4, NW))] * 4,
            dma((8,)), dma((8,)),
            dma, dma, dma((7,)), dma((7,)), dma((15,)), dma((15,)), dma((7,)), dma((7,)), dma, dma,
        ],
        compiler_params=params(54, 1),
        name="front",
    )(*lists, tile_col, omega, idf.reshape(16, T), tiles)


def project_kernel(col, group, slot, live, tiles_ref, w_ref, st_ref, linv_ref, acc, q_ref):
    step = pl.program_id(0)

    @pl.when(step == 0)
    def _():
        @pl.loop(0, 64)
        def _(i):
            acc[i] = jnp.zeros((T, T), F32)

    @pl.loop(0, 2)
    def _(i):
        b = jnp.minimum(2 * step + i, 15)
        q_ref[pl.ds(b * T, T), :] = lax.dot_general(
            st_ref[b], linv_ref[...], (((0,), (1,)), ((), ())), precision=HIGH, preferred_element_type=F32
        )

    @pl.loop(0, STEP, unroll=2)
    def _(i):
        r = step * STEP + i
        tile_row = jnp.concatenate([tiles_ref[i, j] for j in range(5)], axis=1)
        w = w_ref[group[r] * 16 + slot[r]]
        w = jnp.where(r < live[0], w, jnp.zeros_like(w))
        part = jnp.dot(w, tile_row, preferred_element_type=F32)
        for j in range(5):
            c = col[r, j]
            dev, b = c // 4, c % 4
            flow = b // 2
            u, v = dev // 4, dev % 4
            t = jnp.where(flow == 0, u * 4 + v, v * 4 + u)
            acc[flow * 32 + t * 2 + b % 2] += part[:, j * T : (j + 1) * T]


def project(tiles, tile_col, strip_group, strip_slot, live_count, weighted, st, linv):
    strips = tiles.shape[0]
    return pl.pallas_call(
        project_kernel,
        out_shape=(
            jax.ShapeDtypeStruct((64, T, T), F32),
            jax.ShapeDtypeStruct((16 * T, T), F32),
        ),
        grid=(strips // STEP,),
        in_specs=[
            SMEM,
            SMEM,
            SMEM,
            SMEM,
            pl.BlockSpec((STEP, 5, T, T), lambda i: (i, 0, 0, 0)),
            pl.BlockSpec((256, T, T), lambda i: (0, 0, 0)),
            pl.BlockSpec((16, T, T), lambda i: (0, 0, 0)),
            pl.BlockSpec((T, T), lambda i: (0, 0)),
        ],
        out_specs=(
            pl.BlockSpec((64, T, T), lambda i: (0, 0, 0)),
            pl.BlockSpec((16 * T, T), lambda i: (0, 0)),
        ),
        compiler_params=params(48),
        name="project",
    )(tile_col, strip_group, strip_slot, live_count, tiles, weighted.reshape(256, T, T), st, linv)


def ring_sum(at, axis, own, out_refs, in_refs, send, recv, size):
    here = at[axis]
    dtype = out_refs[0].dtype
    low, high = pl.ds(0, size), pl.ds(size, size)
    r0, r1, l0, l1 = range(4)
    sent = []

    def copy(k, src, dst, right):
        return pltpu.make_async_remote_copy(
            src_ref=src,
            dst_ref=dst,
            send_sem=send.at[k],
            recv_sem=recv.at[k],
            device_id=moved(at, axis, 1 if right else -1, 4),
            device_id_type=MESH,
        )

    def fill(k, offset, target, extra=None):
        out = out_refs[k]
        base = 0 if k in (r0, l0) else offset

        @pl.loop(0, size)
        def _(b):
            v = own[target, b + offset]
            if extra is not None:
                v = v + extra[b].astype(F32)
            out[base + b] = v.astype(dtype)

    far = lax.rem(here + 2, 4)
    right, left = lax.rem(here + 1, 4), lax.rem(here + 3, 4)
    c_r0 = copy(0, out_refs[r0], in_refs[r0], True)
    c_l0 = copy(1, out_refs[l0], in_refs[l0], False)
    c_r1q = copy(2, out_refs[r1].at[high], in_refs[r1].at[high], True)
    c_l1p = copy(3, out_refs[l1].at[low], in_refs[l1].at[low], False)
    c_r1p = copy(4, out_refs[r1].at[low], in_refs[r1].at[low], True)
    c_l1q = copy(5, out_refs[l1].at[high], in_refs[l1].at[high], False)
    fill(r0, 0, far)
    c_r0.start()
    fill(l0, size, far)
    c_l0.start()
    yield
    fill(r1, size, right)
    c_r1q.start()
    fill(l1, 0, left)
    c_l1p.start()
    yield
    c_r0.wait_recv()
    fill(r1, 0, right, in_refs[r0])
    c_r1p.start()
    c_l0.wait_recv()
    fill(l1, size, left, in_refs[l0])
    c_l1q.start()
    yield
    for c in (c_r1q, c_l1p, c_r1p, c_l1q):
        c.wait_recv()
    yield
    for c in (c_r0, c_l0, c_r1q, c_l1p, c_r1p, c_l1q):
        c.wait_send()
    yield


def docs_kernel(part_ref, linv_ref, out_ref, *scratch):
    at = place()
    bufs1 = [scratch[0:8], scratch[8:16]]
    bufs2 = [scratch[16:24], scratch[24:32]]
    sums, final, send, recv = scratch[32:]
    greet([moved(at, "x", 1, 4), moved(at, "x", -1, 4), moved(at, "y", 1, 4), moved(at, "y", -1, 4)])
    axes = ("x", "y")
    runs = [
        ring_sum(
            at, axes[f], part_ref.at[f], bufs1[f][:4], bufs1[f][4:], send.at[f], recv.at[f], 4
        )
        for f in range(2)
    ]
    for _ in range(4):
        for run in runs:
            next(run)
    for f in range(2):
        in_r, in_l = bufs1[f][5], bufs1[f][7]
        here = at[axes[f]]

        @pl.loop(0, 8)
        def _(b):
            v = part_ref[f, here, b] + in_r[b].astype(F32) + in_l[b].astype(F32)
            sums[f, b // 2, b % 2] = v

    later = [
        ring_sum(
            at, axes[1 - f], sums.at[f], bufs2[f][:4], bufs2[f][4:], send.at[2 + f], recv.at[2 + f], 1
        )
        for f in range(2)
    ]
    for _ in range(4):
        for run in later:
            next(run)
    for f in range(2):
        in_r, in_l = bufs2[f][5], bufs2[f][7]
        here = at[axes[1 - f]]
        for b in range(2):
            final[2 * f + b] = sums[f, here, b] + in_r[b] + in_l[b]
    for b in range(4):
        out_ref[:, b * T : (b + 1) * T] = jnp.dot(
            linv_ref[...], final[b], precision=HIGH, preferred_element_type=F32
        ).astype(BF16)
    for run in (*runs, *later):
        next(run)


def sum_docs(parts, linv):
    dma = pltpu.SemaphoreType.DMA

    def bufs(size, dtype):
        return [pltpu.VMEM((n * size, T, T), dtype) for n in (1, 2, 1, 2)] * 2

    return pl.pallas_call(
        docs_kernel,
        out_shape=jax.ShapeDtypeStruct((T, 4 * T), BF16),
        in_specs=[VMEM, VMEM],
        out_specs=VMEM,
        scratch_shapes=[
            *bufs(4, BF16),
            *bufs(4, BF16),
            *bufs(1, F32),
            *bufs(1, F32),
            pltpu.VMEM((2, 4, 2, T, T), F32),
            pltpu.VMEM((4, T, T), F32),
            dma((4, 6)),
            dma((4, 6)),
        ],
        compiler_params=params(24, 4),
        name="docs_sum",
    )(parts.reshape(2, 4, 8, T, T), linv)


def on_device(tiles, tile_col, strip_group, strip_slot, live_count, omega, idf):
    terms = idf.shape[0] * 256
    lists = strip_lists(strip_group, strip_slot, live_count)
    weighted, st, linv = front(lists, tile_col, tiles, omega, idf, terms)
    where = (tile_col, strip_group, strip_slot, live_count)
    doc_parts, q_basis = project(tiles, *where, weighted, st, linv)
    doc_factor = sum_docs(doc_parts, linv)
    return q_basis, doc_factor


def solution(mesh):
    torus = Mesh(mesh.devices.reshape(8, 2, 4, 4), AXES)
    in_specs = (
        P(AXES, None, None, None),
        P(AXES, None),
        P(AXES),
        P(AXES),
        P(AXES),
        P(AXES, None),
        P(AXES),
    )
    out_specs = (P(AXES, None), P(None, AXES))
    return jax.shard_map(
        on_device, mesh=torus, in_specs=in_specs, out_specs=out_specs, check_vma=False
    )
```

time: 208 us -> 177 us (0.85)
  waiting for transfers between devices: 14.9 us -> 0 us
  between operations: 14.7 us -> 1.37 us
  local copies, waits for them, and re-layouts: 8.4 us -> 4.12 us
    all_gather x1 -> x0, waiting for transfers between devices: 14.9 us -> none  [on_device(): weighted = lax.all_gather(wt, ('z', 'c'), axis=0, tiled=True)]
    unnamed x18 -> x12, local copies, waits for them, and re-layouts: 8.4 us -> 4.12 us
    pallas_call x6 -> x3, Pallas kernels: 146 us -> 148 us  [the longest x1 122 us: front(): pl.pallas_call(functools.partial(front_kernel, terms), out_shape=(jax.Sha...]
  transfers between devices with their start and end apart: 1 -> 0, of which waited for: 1 -> 0; matrix products, arithmetic and copies ran while one was open for 0% -> 0% of each run, Pallas kernels for 19% -> 0%
where the time goes in v2:
time: 177 us; the launch traced here: 176 us
  Pallas kernels  171 us (97%)
  local copies, waits for them, and re-layouts  4.12 us (2%)
    pallas_call x1, Pallas kernels, front(): pl.pallas_call(functools.partial(front_kernel, terms), out_shape=(jax.Sha...  122 us
    pallas_call x1, Pallas kernels, project(): pl.pallas_call(project_kernel, out_shape=(jax.ShapeDtypeStruct((64, T, T)...  24.1 us
    pallas_call x1, Pallas kernels, sum_docs(): pl.pallas_call(docs_kernel, out_shape=jax.ShapeDtypeStruct((T, 4 * T), BF...  22.2 us
    unnamed x12, local copies, waits for them, and re-layouts  4.12 us

profile of v2, /device:TPU:2, one launch (start us, length us, event | category | flops | bytes accessed | tf_op | source)
XLA Modules:
  0.0 176.2 jit_solution(4413416363450776644)
XLA Ops:
  0.6 0.0 copy-start.4
  0.6 0.0 copy-start.3
  1.3 2.7 %strip_lists.1 = (s32[96]{0:T(128)}, s32[96]{0:T(128)}, s32[256]{0:T(256)}) custom-call(s32[72]{0:T(128)} %group.3, s32[72]{0:T(128)} %slot.3, s32[1]{0:T(128)S(6)} %copy.12.live), custom_call_target="tpu_custom_call" | custom-call | tf_op jit(solution)/shard_map/strip_lists/pallas_call | solution.py:82
  4.0 1.4 copy.10.col
  5.4 0.0 copy-start.1
  5.4 121.7 %front.1 = (bf16[16,16,128,128]{3,2,1,0:T(8,128)(2,1)}, f32[16,128,128]{2,1,0:T(8,128)}, f32[128,128]{1,0:T(8,128)}) custom-call(s32[96]{0:T(128)} %get-tuple-element.10.strip, s32[96]{0:T(128)} %get-tuple-element.11.before, s32[256]{0:T(256)} %get-tuple-element.12.last, s32[72,5]{1,0:T(8,128)} %copy.10.col, bf16[512,128]{1,0:T(8,128)(2,1)} %omega_ref.1, ...), custom_call_target="tpu_custom_call" | custom-call | tf_op jit(solution)/shard_map/front/pallas_call | solution.py:471
  127.1 0.0 copy-done.4
  127.1 0.0 copy-done.3
  127.2 0.0 copy-done.1
  127.2 0.0 copy-start
  127.2 1.2 copy-done
  128.4 0.0 copy-start.2
  128.4 0.8 copy-done.2
  129.2 24.1 %project.1 = (f32[64,128,128]{2,1,0:T(8,128)S(1)}, f32[2048,128]{1,0:T(8,128)}) custom-call(s32[72,5]{1,0:T(8,128)S(1)} %copy-done.1, s32[72]{0:T(128)S(1)} %copy-done.3, s32[72]{0:T(128)S(1)} %copy-done.4, s32[1]{0:T(128)S(6)} %copy.12.live, bf16[72,5,128,128]{3,2,1,0:T(8,128)(2,1)} %tiles_ref.3, bf16[256,128,128]{2,1,0:T(8,128)(2,1)} %bitcast.4, ...), custom_call_target="tpu_custom_call" | custom-call | tf_op jit(solution)/shard_map/project/pallas_call | solution.py:546
  153.3 22.2 %docs_sum.1 = bf16[128,512]{1,0:T(8,128)(2,1)S(1)} custom-call(f32[2,4,8,128,128]{4,3,2,1,0:T(8,128)S(1)} %bitcast.3, f32[128,128]{1,0:T(8,128)S(1)} %copy-done.2), custom_call_target="tpu_custom_call" | custom-call | tf_op jit(solution)/shard_map/docs_sum/pallas_call | solution.py:686
  175.5 0.7 copy.13
Async XLA Ops:
  0.6 126.5 %copy-start.4 = (s32[72]{0:T(128)S(1)}, s32[72]{0:T(128)}, u32[]{:S(2)}) copy-start(s32[72]{0:T(128)} %slot.3) | copy-start | bytes 868
  0.6 126.5 %copy-start.3 = (s32[72]{0:T(128)S(1)}, s32[72]{0:T(128)}, u32[]{:S(2)}) copy-start(s32[72]{0:T(128)} %group.3) | copy-start | bytes 868
  5.4 121.7 %copy-start.1 = (s32[72,5]{1,0:T(8,128)S(1)}, s32[72,5]{1,0:T(8,128)}, u32[]{:S(2)}) copy-start(s32[72,5]{1,0:T(8,128)} %copy.10.col) | copy-start | bytes 4324
  127.2 1.2 copy-start
  128.4 0.8 copy-start.2

commit v3 on v2

--- a/solution.py
+++ b/solution.py
@@ -265,7 +265,8 @@
     me = at["x"] * 4 + at["y"]
     for b in range(4):
         om[me * 4 + b] = omega_ref[b * T : (b + 1) * T, :].T
-    greet([sibling, *[moved(at, "z", d, NZ) for d in range(1, NZ)], *xy_others(at)])
+    near = [moved(at, a, d, 4) for a in ("x", "y") for d in (1, -1)]
+    greet([sibling, *near, moved(at, "z", 1, NZ), moved(at, "z", -1, NZ)])
     sent = gather_omega(at, omega_ref, om, om_send, om_recv)
 
     @pl.loop(0, 2 * (PER + 1))
@@ -286,7 +287,7 @@
             def _(n):
                 i = strip[o * PER + n]
                 tile_row = jnp.concatenate([tiles[i, j] for j in range(5)], axis=1)
-                m = jnp.concatenate([om[col[i, j]] for j in range(5)], axis=1)
+                m = jnp.concatenate([om[col[j, i]] for j in range(5)], axis=1)
                 raw[k * PER + n] = lax.dot_general(m, tile_row, NT, preferred_element_type=F32)
 
             @pl.loop(0, PER)
@@ -432,9 +433,11 @@
         gram[...] += lax.dot_general(v, v, NT, precision=HIGH, preferred_element_type=F32)
 
     def side():
-        yield from gram_steps(
+        for _ in gram_steps(
             at, gram, whole, half, from_sib, over_z, piece, over_xy, total, gram_sems
-        )
+        ):
+            yield
+            yield
         yield from eliminate(terms, whole, linv_ref, work, pivots)
 
     aside = side()
@@ -448,8 +451,7 @@
             wcopy(False, hop - 1, sub).wait_recv()
             if hop < 4 or sub >= NW // 2:
                 wgo(False, hop, sub)
-            if n % 2 == 1:
-                next(aside, None)
+            next(aside, None)
         to_sibling(hop - 1)
         to_sibling(NZ - (hop - 1))
     for _ in aside:
@@ -509,7 +511,7 @@
     )(*lists, tile_col, omega, idf.reshape(16, T), tiles)
 
 
-def project_kernel(col, group, slot, live, tiles_ref, w_ref, st_ref, linv_ref, acc, q_ref):
+def project_kernel(col, group, slot, live, tiles_ref, w_ref, acc, raw):
     step = pl.program_id(0)
 
     @pl.when(step == 0)
@@ -518,37 +520,28 @@
         def _(i):
             acc[i] = jnp.zeros((T, T), F32)
 
-    @pl.loop(0, 2)
-    def _(i):
-        b = jnp.minimum(2 * step + i, 15)
-        q_ref[pl.ds(b * T, T), :] = lax.dot_general(
-            st_ref[b], linv_ref[...], (((0,), (1,)), ((), ())), precision=HIGH, preferred_element_type=F32
-        )
-
-    @pl.loop(0, STEP, unroll=2)
-    def _(i):
+    for i in range(STEP):
         r = step * STEP + i
         tile_row = jnp.concatenate([tiles_ref[i, j] for j in range(5)], axis=1)
         w = w_ref[group[r] * 16 + slot[r]]
         w = jnp.where(r < live[0], w, jnp.zeros_like(w))
-        part = jnp.dot(w, tile_row, preferred_element_type=F32)
+        raw[i] = jnp.dot(w, tile_row, preferred_element_type=F32)
+    for i in range(STEP):
+        r = step * STEP + i
         for j in range(5):
-            c = col[r, j]
+            c = col[j, r]
             dev, b = c // 4, c % 4
             flow = b // 2
             u, v = dev // 4, dev % 4
             t = jnp.where(flow == 0, u * 4 + v, v * 4 + u)
-            acc[flow * 32 + t * 2 + b % 2] += part[:, j * T : (j + 1) * T]
-
-
-def project(tiles, tile_col, strip_group, strip_slot, live_count, weighted, st, linv):
+            acc[flow * 32 + t * 2 + b % 2] += raw[i, :, j * T : (j + 1) * T]
+
+
+def project(tiles, tile_col, strip_group, strip_slot, live_count, weighted):
     strips = tiles.shape[0]
     return pl.pallas_call(
         project_kernel,
-        out_shape=(
-            jax.ShapeDtypeStruct((64, T, T), F32),
-            jax.ShapeDtypeStruct((16 * T, T), F32),
-        ),
+        out_shape=jax.ShapeDtypeStruct((64, T, T), F32),
         grid=(strips // STEP,),
         in_specs=[
             SMEM,
@@ -557,16 +550,12 @@
             SMEM,
             pl.BlockSpec((STEP, 5, T, T), lambda i: (i, 0, 0, 0)),
             pl.BlockSpec((256, T, T), lambda i: (0, 0, 0)),
-            pl.BlockSpec((16, T, T), lambda i: (0, 0, 0)),
-            pl.BlockSpec((T, T), lambda i: (0, 0)),
         ],
-        out_specs=(
-            pl.BlockSpec((64, T, T), lambda i: (0, 0, 0)),
-            pl.BlockSpec((16 * T, T), lambda i: (0, 0)),
-        ),
+        out_specs=pl.BlockSpec((64, T, T), lambda i: (0, 0, 0)),
+        scratch_shapes=[pltpu.VMEM((STEP, T, 5 * T), F32)],
         compiler_params=params(48),
         name="project",
-    )(tile_col, strip_group, strip_slot, live_count, tiles, weighted.reshape(256, T, T), st, linv)
+    )(tile_col, strip_group, strip_slot, live_count, tiles, weighted.reshape(256, T, T))
 
 
 def ring_sum(at, axis, own, out_refs, in_refs, send, recv, size):
@@ -630,7 +619,7 @@
     yield
 
 
-def docs_kernel(part_ref, linv_ref, out_ref, *scratch):
+def docs_kernel(part_ref, linv_ref, st_ref, out_ref, q_ref, *scratch):
     at = place()
     bufs1 = [scratch[0:8], scratch[8:16]]
     bufs2 = [scratch[16:24], scratch[24:32]]
@@ -643,9 +632,23 @@
         )
         for f in range(2)
     ]
-    for _ in range(4):
+    for _ in range(2):
         for run in runs:
             next(run)
+
+    def basis(first, end):
+        @pl.loop(first, end)
+        def _(b):
+            q_ref[pl.ds(b * T, T), :] = lax.dot_general(
+                st_ref[b], linv_ref[...], (((0,), (1,)), ((), ())), precision=HIGH, preferred_element_type=F32
+            )
+
+    basis(0, 6)
+    for run in runs:
+        next(run)
+    basis(6, 12)
+    for run in runs:
+        next(run)
     for f in range(2):
         in_r, in_l = bufs1[f][5], bufs1[f][7]
         here = at[axes[f]]
@@ -661,14 +664,18 @@
         )
         for f in range(2)
     ]
-    for _ in range(4):
+    for _ in range(2):
+        for run in later:
+            next(run)
+    basis(12, 16)
+    for _ in range(2):
         for run in later:
             next(run)
     for f in range(2):
         in_r, in_l = bufs2[f][5], bufs2[f][7]
         here = at[axes[1 - f]]
         for b in range(2):
-            final[2 * f + b] = sums[f, here, b] + in_r[b] + in_l[b]
+            final[2 * f + b] = sums[f, here, b] + in_r[b].astype(F32) + in_l[b].astype(F32)
     for b in range(4):
         out_ref[:, b * T : (b + 1) * T] = jnp.dot(
             linv_ref[...], final[b], precision=HIGH, preferred_element_type=F32
@@ -677,7 +684,7 @@
         next(run)
 
 
-def sum_docs(parts, linv):
+def sum_docs(parts, linv, st):
     dma = pltpu.SemaphoreType.DMA
 
     def bufs(size, dtype):
@@ -685,14 +692,17 @@
 
     return pl.pallas_call(
         docs_kernel,
-        out_shape=jax.ShapeDtypeStruct((T, 4 * T), BF16),
-        in_specs=[VMEM, VMEM],
-        out_specs=VMEM,
+        out_shape=(
+            jax.ShapeDtypeStruct((T, 4 * T), BF16),
+            jax.ShapeDtypeStruct((16 * T, T), F32),
+        ),
+        in_specs=[VMEM, VMEM, VMEM],
+        out_specs=(VMEM, VMEM),
         scratch_shapes=[
             *bufs(4, BF16),
             *bufs(4, BF16),
-            *bufs(1, F32),
-            *bufs(1, F32),
+            *bufs(1, BF16),
+            *bufs(1, BF16),
             pltpu.VMEM((2, 4, 2, T, T), F32),
             pltpu.VMEM((4, T, T), F32),
             dma((4, 6)),
@@ -700,16 +710,17 @@
         ],
         compiler_params=params(24, 4),
         name="docs_sum",
-    )(parts.reshape(2, 4, 8, T, T), linv)
+    )(parts.reshape(2, 4, 8, T, T), linv, st)
 
 
 def on_device(tiles, tile_col, strip_group, strip_slot, live_count, omega, idf):
     terms = idf.shape[0] * 256
     lists = strip_lists(strip_group, strip_slot, live_count)
+    tile_col = tile_col.T
     weighted, st, linv = front(lists, tile_col, tiles, omega, idf, terms)
     where = (tile_col, strip_group, strip_slot, live_count)
-    doc_parts, q_basis = project(tiles, *where, weighted, st, linv)
-    doc_factor = sum_docs(doc_parts, linv)
+    doc_parts = project(tiles, *where, weighted)
+    doc_factor, q_basis = sum_docs(doc_parts, linv, st)
     return q_basis, doc_factor
 
 

time: 177 us -> 167 us (0.944)
  Pallas kernels: 171 us -> 164 us
  local copies, waits for them, and re-layouts: 4.12 us -> 1.65 us
    pallas_call x2, Pallas kernels: 46.3 us -> 36.6 us  [the longest x1 21.9 us: sum_docs(): pl.pallas_call(docs_kernel, out_shape=(jax.ShapeDtypeStruct((T, 4 * T), B...]
    pallas_call x1, Pallas kernels: 122 us -> 124 us  [front(): pl.pallas_call(functools.partial(front_kernel, terms), out_shape=(jax.Sha...]
    unnamed x12, local copies, waits for them, and re-layouts: 4.12 us -> 1.65 us
where the time goes in v3:
time: 167 us
  Pallas kernels  164 us (98%)
    pallas_call x1, Pallas kernels, front(): pl.pallas_call(functools.partial(front_kernel, terms), out_shape=(jax.Sha...  124 us
    pallas_call x1, Pallas kernels, sum_docs(): pl.pallas_call(docs_kernel, out_shape=(jax.ShapeDtypeStruct((T, 4 * T), B...  21.9 us
    pallas_call x1, Pallas kernels, project(): pl.pallas_call(project_kernel, out_shape=jax.ShapeDtypeStruct((64, T, T),...  14.8 us

profile of v3, /device:TPU:2, one launch (start us, length us, event | category | flops | bytes accessed | tf_op | source)
XLA Modules:
  0.0 166.6 jit_solution(2586651999888994801)
XLA Ops:
  0.6 0.0 copy-start.4
  0.6 0.0 copy-start.3
  0.7 0.0 copy-start.2
  1.3 2.5 %strip_lists.1 = (s32[96]{0:T(128)}, s32[96]{0:T(128)}, s32[256]{0:T(256)}) custom-call(s32[72]{0:T(128)} %group.3, s32[72]{0:T(128)} %slot.3, s32[1]{0:T(128)S(6)} %copy.11.live), custom_call_target="tpu_custom_call" | custom-call | tf_op jit(solution)/shard_map/strip_lists/pallas_call | solution.py:82
  3.8 124.4 %front.1 = (bf16[16,16,128,128]{3,2,1,0:T(8,128)(2,1)}, f32[16,128,128]{2,1,0:T(8,128)}, f32[128,128]{1,0:T(8,128)}) custom-call(s32[96]{0:T(128)} %get-tuple-element.10.strip, s32[96]{0:T(128)} %get-tuple-element.11.before, s32[256]{0:T(256)} %get-tuple-element.12.last, s32[5,72]{1,0:T(8,128)} %bitcast.5, bf16[512,128]{1,0:T(8,128)(2,1)} %omega_ref.1, ...), custom_call_target="tpu_custom_call" | custom-call | tf_op jit(solution)/shard_map/front/pallas_call | solution.py:473
  128.3 0.0 copy-done.4
  128.3 0.0 copy-done.3
  128.3 0.0 copy-done.2
  128.3 0.0 copy-start
  128.3 0.0 copy-start.1
  128.3 14.8 %project.1 = f32[64,128,128]{2,1,0:T(8,128)S(1)} custom-call(s32[5,72]{1,0:T(8,128)S(1)} %bitcast.6, s32[72]{0:T(128)S(1)} %copy-done.3, s32[72]{0:T(128)S(1)} %copy-done.4, s32[1]{0:T(128)S(6)} %copy.11.live, bf16[72,5,128,128]{3,2,1,0:T(8,128)(2,1)} %tiles_ref.3, bf16[256,128,128]{2,1,0:T(8,128)(2,1)} %bitcast.7), custom_call_target="tpu_custom_call" | custom-call | tf_op jit(solution)/shard_map/project/pallas_call | solution.py:542
  143.1 0.0 copy-done
  143.1 0.0 copy-done.1
  143.1 21.9 %docs_sum.1 = (bf16[128,512]{1,0:T(8,128)(2,1)S(1)}, f32[2048,128]{1,0:T(8,128)S(1)}) custom-call(f32[2,4,8,128,128]{4,3,2,1,0:T(8,128)S(1)} %bitcast.4, f32[128,128]{1,0:T(8,128)S(1)} %copy-done.1, f32[16,128,128]{2,1,0:T(8,128)S(1)} %copy-done), custom_call_target="tpu_custom_call" | custom-call | tf_op jit(solution)/shard_map/docs_sum/pallas_call | solution.py:693
  165.0 1.0 copy.12
  166.0 0.7 copy.13
Async XLA Ops:
  0.6 127.6 %copy-start.4 = (s32[72]{0:T(128)S(1)}, s32[72]{0:T(128)}, u32[]{:S(2)}) copy-start(s32[72]{0:T(128)} %slot.3) | copy-start | bytes 868
  0.6 127.6 %copy-start.3 = (s32[72]{0:T(128)S(1)}, s32[72]{0:T(128)}, u32[]{:S(2)}) copy-start(s32[72]{0:T(128)} %group.3) | copy-start | bytes 868
  0.7 127.6 %copy-start.2 = (s32[72,5]{0,1:T(8,128)S(1)}, s32[72,5]{0,1:T(8,128)}, u32[]{:S(2)}) copy-start(s32[72,5]{0,1:T(8,128)} %param.8) | copy-start | bytes 4324
  128.3 14.8 %copy-start = (f32[16,128,128]{2,1,0:T(8,128)S(1)}, f32[16,128,128]{2,1,0:T(8,128)}, u32[]{:S(2)}) copy-start(f32[16,128,128]{2,1,0:T(8,128)} %get-tuple-element.15.st_ref) | copy-start | bytes 3145732
  128.3 14.8 %copy-start.1 = (f32[128,128]{1,0:T(8,128)S(1)}, f32[128,128]{1,0:T(8,128)}, u32[]{:S(2)}) copy-start(f32[128,128]{1,0:T(8,128)} %get-tuple-element.14.linv_ref) | copy-start | bytes 196612

commit v4 on v3

--- a/solution.py
+++ b/solution.py
@@ -228,33 +228,34 @@
     return [(z, c, lax.rem(x + i, 4), lax.rem(y + j, 4)) for i in range(4) for j in range(4) if i or j]
 
 
-def eliminate(terms, gram, linv_ref, work, pivots):
-    work[:, :T] = gram[...] * (1.0 / terms)
+def eliminate(terms, gram, linv_ref, work):
+    work[...] = gram[...] * (1.0 / terms)
     row = lax.broadcasted_iota(jnp.int32, (T, T), 0)
     lane = lax.broadcasted_iota(jnp.int32, (T, T), 1)
-    work[:, T:] = (row == lane).astype(F32)
-    pivots[...] = jnp.zeros((T, T), F32)
-    for first in range(0, T, 16):
-
-        @pl.loop(first, first + 16)
+    for first in range(0, T, 8):
+
+        @pl.loop(first, first + 8)
         def _(j):
+            here = lane == j
             line = work[pl.ds(j, 1), :]
-            pivot = jnp.sum(jnp.where(lane[:1] == j, line[:, :T], 0.0), axis=1, keepdims=True)
-            scaled = line / pivot
-            column = jnp.sum(jnp.where(lane == j, work[:, :T], 0.0), axis=1, keepdims=True)
-            column = jnp.where(row[:, :1] > j, column, 0.0)
-            work[...] = work[...] - column * scaled
-            pivots[pl.ds(j, 1), :] = jnp.broadcast_to(pivot, (1, T))
+            pivot = jnp.sum(jnp.where(here[:1], line, 0.0), axis=1, keepdims=True)
+            scaled = jnp.where(here[:1], 1.0, line) / pivot
+            block = work[...]
+            column = jnp.sum(jnp.where(here, block, 0.0), axis=1, keepdims=True)
+            below = row > j
+            work[...] = jnp.where(here & below, 0.0, block) - jnp.where(below, column, 0.0) * scaled
 
         yield
-    linv_ref[...] = work[:, T:] * lax.rsqrt(pivots[...])
+    block = work[...]
+    pivots = jnp.sum(jnp.where(lane == row, block, 0.0), axis=1, keepdims=True)
+    linv_ref[...] = jnp.where(lane < row, block, (lane == row).astype(F32)) * lax.rsqrt(pivots)
     yield
 
 
 def front_kernel(
     terms, strip, before, last, col, omega_ref, idf_ref, tiles_ref, w_ref, st_ref, linv_ref,
     tiles, om, raw, chain, own, out_sib, sib, out_r, out_l, in_r, in_l, wt, gram,
-    whole, half, from_sib, over_z, piece, over_xy, total, work, pivots,
+    whole, half, from_sib, over_z, piece, over_xy, total, work,
     load_sem, om_send, om_recv, sib_send, sib_recv, r_send, r_recv, l_send, l_recv,
     own_sem, wr_send, wr_recv, wl_send, wl_recv, ws_send, ws_recv, *gram_sems,
 ):
@@ -438,7 +439,7 @@
         ):
             yield
             yield
-        yield from eliminate(terms, whole, linv_ref, work, pivots)
+        yield from eliminate(terms, whole, linv_ref, work)
 
     aside = side()
     next(aside)
@@ -495,7 +496,6 @@
             v((8, T), F32),
             v((16, 8, T), F32),
             v((64, T), F32),
-            v((T, 2 * T), F32),
             v((T, T), F32),
             dma,
             dma((10, 4)), dma((10, 4)),
@@ -511,8 +511,30 @@
     )(*lists, tile_col, omega, idf.reshape(16, T), tiles)
 
 
-def project_kernel(col, group, slot, live, tiles_ref, w_ref, acc, raw):
+def project_kernel(col, group, slot, live, tiles_ref, w_ref, acc, raw, blocks, sem):
     step = pl.program_id(0)
+
+    def fetch(step):
+        at = step % 2
+        copies = []
+        for i in range(STEP):
+            r = step * STEP + i
+            copies.append(
+                pltpu.make_async_copy(
+                    w_ref.at[group[r] * 16 + slot[r]], blocks.at[at, i], sem.at[at, i]
+                )
+            )
+        return copies
+
+    @pl.when(step == 0)
+    def _():
+        for c in fetch(step):
+            c.start()
+
+    @pl.when(step + 1 < pl.num_programs(0))
+    def _():
+        for c in fetch(step + 1):
+            c.start()
 
     @pl.when(step == 0)
     def _():
@@ -520,10 +542,12 @@
         def _(i):
             acc[i] = jnp.zeros((T, T), F32)
 
+    for c in fetch(step):
+        c.wait()
     for i in range(STEP):
         r = step * STEP + i
         tile_row = jnp.concatenate([tiles_ref[i, j] for j in range(5)], axis=1)
-        w = w_ref[group[r] * 16 + slot[r]]
+        w = blocks[step % 2, i]
         w = jnp.where(r < live[0], w, jnp.zeros_like(w))
         raw[i] = jnp.dot(w, tile_row, preferred_element_type=F32)
     for i in range(STEP):
@@ -549,10 +573,14 @@
             SMEM,
             SMEM,
             pl.BlockSpec((STEP, 5, T, T), lambda i: (i, 0, 0, 0)),
-            pl.BlockSpec((256, T, T), lambda i: (0, 0, 0)),
+            ANY,
         ],
         out_specs=pl.BlockSpec((64, T, T), lambda i: (0, 0, 0)),
-        scratch_shapes=[pltpu.VMEM((STEP, T, 5 * T), F32)],
+        scratch_shapes=[
+            pltpu.VMEM((STEP, T, 5 * T), F32),
+            pltpu.VMEM((2, STEP, T, T), BF16),
+            pltpu.SemaphoreType.DMA((2, STEP)),
+        ],
         compiler_params=params(48),
         name="project",
     )(tile_col, strip_group, strip_slot, live_count, tiles, weighted.reshape(256, T, T))

time: 167 us -> 161 us (0.964)
  Pallas kernels: 164 us -> 158 us
    pallas_call x1, Pallas kernels: 124 us -> 120 us  [front(): pl.pallas_call(functools.partial(front_kernel, terms), out_shape=(jax.Sha...]
where the time goes in v4:
time: 161 us
  Pallas kernels  158 us (98%)
  local copies, waits for them, and re-layouts  1.65 us (1%)
    pallas_call x1, Pallas kernels, front(): pl.pallas_call(functools.partial(front_kernel, terms), out_shape=(jax.Sha...  120 us
    pallas_call x1, Pallas kernels, sum_docs(): pl.pallas_call(docs_kernel, out_shape=(jax.ShapeDtypeStruct((T, 4 * T), B...  21.7 us
    pallas_call x1, Pallas kernels, project(): pl.pallas_call(project_kernel, out_shape=jax.ShapeDtypeStruct((64, T, T),...  13.1 us

profile of v4, /device:TPU:2, one launch (start us, length us, event | category | flops | bytes accessed | tf_op | source)
XLA Modules:
  0.0 160.7 jit_solution(8258581531816593626)
XLA Ops:
  0.6 0.0 copy-start.4
  0.6 0.0 copy-start.3
  0.7 0.0 copy-start.2
  1.3 2.5 %strip_lists.1 = (s32[96]{0:T(128)}, s32[96]{0:T(128)}, s32[256]{0:T(256)}) custom-call(s32[72]{0:T(128)} %group.3, s32[72]{0:T(128)} %slot.3, s32[1]{0:T(128)S(6)} %copy.11.live), custom_call_target="tpu_custom_call" | custom-call | tf_op jit(solution)/shard_map/strip_lists/pallas_call | solution.py:82
  3.8 120.3 %front.1 = (bf16[16,16,128,128]{3,2,1,0:T(8,128)(2,1)}, f32[16,128,128]{2,1,0:T(8,128)}, f32[128,128]{1,0:T(8,128)}) custom-call(s32[96]{0:T(128)} %get-tuple-element.10.strip, s32[96]{0:T(128)} %get-tuple-element.11.before, s32[256]{0:T(256)} %get-tuple-element.12.last, s32[5,72]{1,0:T(8,128)} %bitcast.5, bf16[512,128]{1,0:T(8,128)(2,1)} %omega_ref.1, ...), custom_call_target="tpu_custom_call" | custom-call | tf_op jit(solution)/shard_map/front/pallas_call | solution.py:474
  124.1 0.0 copy-done.4
  124.1 0.0 copy-done.3
  124.1 0.0 copy-done.2
  124.2 0.0 copy-start
  124.2 0.0 copy-start.1
  124.2 13.1 %project.1 = f32[64,128,128]{2,1,0:T(8,128)S(1)} custom-call(s32[5,72]{1,0:T(8,128)S(1)} %bitcast.6, s32[72]{0:T(128)S(1)} %copy-done.3, s32[72]{0:T(128)S(1)} %copy-done.4, s32[1]{0:T(128)S(6)} %copy.11.live, bf16[72,5,128,128]{3,2,1,0:T(8,128)(2,1)} %tiles_ref.3, bf16[256,128,128]{2,1,0:T(8,128)(2,1)} %bitcast.7), custom_call_target="tpu_custom_call" | custom-call | tf_op jit(solution)/shard_map/project/pallas_call | solution.py:566
  137.3 0.0 copy-done
  137.3 0.0 copy-done.1
  137.3 21.7 %docs_sum.1 = (bf16[128,512]{1,0:T(8,128)(2,1)S(1)}, f32[2048,128]{1,0:T(8,128)S(1)}) custom-call(f32[2,4,8,128,128]{4,3,2,1,0:T(8,128)S(1)} %bitcast.4, f32[128,128]{1,0:T(8,128)S(1)} %copy-done.1, f32[16,128,128]{2,1,0:T(8,128)S(1)} %copy-done), custom_call_target="tpu_custom_call" | custom-call | tf_op jit(solution)/shard_map/docs_sum/pallas_call | solution.py:721
  159.0 1.0 copy.12
  160.0 0.7 copy.13
Async XLA Ops:
  0.6 123.5 %copy-start.4 = (s32[72]{0:T(128)S(1)}, s32[72]{0:T(128)}, u32[]{:S(2)}) copy-start(s32[72]{0:T(128)} %slot.3) | copy-start | bytes 868
  0.6 123.5 %copy-start.3 = (s32[72]{0:T(128)S(1)}, s32[72]{0:T(128)}, u32[]{:S(2)}) copy-start(s32[72]{0:T(128)} %group.3) | copy-start | bytes 868
  0.7 123.5 %copy-start.2 = (s32[72,5]{0,1:T(8,128)S(1)}, s32[72,5]{0,1:T(8,128)}, u32[]{:S(2)}) copy-start(s32[72,5]{0,1:T(8,128)} %param.8) | copy-start | bytes 4324
  124.2 13.1 %copy-start = (f32[16,128,128]{2,1,0:T(8,128)S(1)}, f32[16,128,128]{2,1,0:T(8,128)}, u32[]{:S(2)}) copy-start(f32[16,128,128]{2,1,0:T(8,128)} %get-tuple-element.15.st_ref) | copy-start | bytes 3145732
  124.2 13.1 %copy-start.1 = (f32[128,128]{1,0:T(8,128)S(1)}, f32[128,128]{1,0:T(8,128)}, u32[]{:S(2)}) copy-start(f32[128,128]{1,0:T(8,128)} %get-tuple-element.14.linv_ref) | copy-start | bytes 196612

commit v5 on v4

--- a/solution.py
+++ b/solution.py
@@ -47,7 +47,7 @@
     )
 
 
-STEP = 8
+STEP = 12
 PER = 6
 NONE = 6
 
@@ -95,8 +95,8 @@
 
 ORDER = (4, 3, 5, 2, 6, 1, 7, 0)
 SUB = 4
-SUBW = 2
-NW = 8
+SUBW = 4
+NW = 4
 
 
 def gather_omega(at, omega_ref, om, send, recv):
@@ -284,18 +284,18 @@
             o = 2 * z + (1 - at["c"] if k == 0 else at["c"])
             base = k * (PER + 1)
 
-            @pl.loop(0, PER, unroll=3)
+            @pl.loop(0, PER, unroll=6)
             def _(n):
                 i = strip[o * PER + n]
                 tile_row = jnp.concatenate([tiles[i, j] for j in range(5)], axis=1)
                 m = jnp.concatenate([om[col[j, i]] for j in range(5)], axis=1)
                 raw[k * PER + n] = lax.dot_general(m, tile_row, NT, preferred_element_type=F32)
 
-            @pl.loop(0, PER)
+            @pl.loop(0, PER, unroll=2)
             def _(n):
                 chain[base + n] = raw[k * PER + n] + chain[base + before[o * PER + n]]
 
-            @pl.loop(0, 16, unroll=2)
+            @pl.loop(0, 16, unroll=4)
             def _(b):
                 target[q, b] = chain[base + last[o * 16 + b]].astype(BF16)
 
@@ -443,7 +443,7 @@
 
     aside = side()
     next(aside)
-    order = (4, 5, 6, 7, 0, 1, 2, 3)
+    order = (2, 3, 0, 1)
     for hop in (2, 3, 4):
         for n, sub in enumerate(order):
             wcopy(True, hop - 1, sub).wait_recv()
@@ -452,6 +452,7 @@
             wcopy(False, hop - 1, sub).wait_recv()
             if hop < 4 or sub >= NW // 2:
                 wgo(False, hop, sub)
+            next(aside, None)
             next(aside, None)
         to_sibling(hop - 1)
         to_sibling(NZ - (hop - 1))

time: 161 us -> 158 us (0.981)
  Pallas kernels: 158 us -> 155 us
where the time goes in v5:
time: 158 us
  Pallas kernels  155 us (98%)
  local copies, waits for them, and re-layouts  1.65 us (1%)
    pallas_call x1, Pallas kernels, front(): pl.pallas_call(functools.partial(front_kernel, terms), out_shape=(jax.Sha...  119 us
    pallas_call x1, Pallas kernels, sum_docs(): pl.pallas_call(docs_kernel, out_shape=(jax.ShapeDtypeStruct((T, 4 * T), B...  21.8 us
    pallas_call x1, Pallas kernels, project(): pl.pallas_call(project_kernel, out_shape=jax.ShapeDtypeStruct((64, T, T),...  11.9 us

profile of v5, /device:TPU:2, one launch (start us, length us, event | category | flops | bytes accessed | tf_op | source)
XLA Modules:
  0.0 158.1 jit_solution(865062235958765243)
XLA Ops:
  0.6 0.0 copy-start.4
  0.6 0.0 copy-start.3
  0.7 0.0 copy-start.2
  1.3 2.5 %strip_lists.1 = (s32[96]{0:T(128)}, s32[96]{0:T(128)}, s32[256]{0:T(256)}) custom-call(s32[72]{0:T(128)} %group.3, s32[72]{0:T(128)} %slot.3, s32[1]{0:T(128)S(6)} %copy.11.live), custom_call_target="tpu_custom_call" | custom-call | tf_op jit(solution)/shard_map/strip_lists/pallas_call | solution.py:82
  3.8 118.9 %front.1 = (bf16[16,16,128,128]{3,2,1,0:T(8,128)(2,1)}, f32[16,128,128]{2,1,0:T(8,128)}, f32[128,128]{1,0:T(8,128)}) custom-call(s32[96]{0:T(128)} %get-tuple-element.10.strip, s32[96]{0:T(128)} %get-tuple-element.11.before, s32[256]{0:T(256)} %get-tuple-element.12.last, s32[5,72]{1,0:T(8,128)} %bitcast.5, bf16[512,128]{1,0:T(8,128)(2,1)} %omega_ref.1, ...), custom_call_target="tpu_custom_call" | custom-call | tf_op jit(solution)/shard_map/front/pallas_call | solution.py:475
  122.8 0.0 copy-done.4
  122.8 0.0 copy-done.3
  122.8 0.0 copy-done.2
  122.8 0.0 copy-start
  122.8 0.0 copy-start.1
  122.8 11.9 %project.1 = f32[64,128,128]{2,1,0:T(8,128)S(1)} custom-call(s32[5,72]{1,0:T(8,128)S(1)} %bitcast.6, s32[72]{0:T(128)S(1)} %copy-done.3, s32[72]{0:T(128)S(1)} %copy-done.4, s32[1]{0:T(128)S(6)} %copy.11.live, bf16[72,5,128,128]{3,2,1,0:T(8,128)(2,1)} %tiles_ref.3, bf16[256,128,128]{2,1,0:T(8,128)(2,1)} %bitcast.7), custom_call_target="tpu_custom_call" | custom-call | tf_op jit(solution)/shard_map/project/pallas_call | solution.py:567
  134.7 0.0 copy-done
  134.7 0.0 copy-done.1
  134.7 21.8 %docs_sum.1 = (bf16[128,512]{1,0:T(8,128)(2,1)S(1)}, f32[2048,128]{1,0:T(8,128)S(1)}) custom-call(f32[2,4,8,128,128]{4,3,2,1,0:T(8,128)S(1)} %bitcast.4, f32[128,128]{1,0:T(8,128)S(1)} %copy-done.1, f32[16,128,128]{2,1,0:T(8,128)S(1)} %copy-done), custom_call_target="tpu_custom_call" | custom-call | tf_op jit(solution)/shard_map/docs_sum/pallas_call | solution.py:722
  156.5 1.0 copy.12
  157.5 0.7 copy.13
Async XLA Ops:
  0.6 122.1 %copy-start.4 = (s32[72]{0:T(128)S(1)}, s32[72]{0:T(128)}, u32[]{:S(2)}) copy-start(s32[72]{0:T(128)} %slot.3) | copy-start | bytes 868
  0.6 122.1 %copy-start.3 = (s32[72]{0:T(128)S(1)}, s32[72]{0:T(128)}, u32[]{:S(2)}) copy-start(s32[72]{0:T(128)} %group.3) | copy-start | bytes 868
  0.7 122.1 %copy-start.2 = (s32[72,5]{0,1:T(8,128)S(1)}, s32[72,5]{0,1:T(8,128)}, u32[]{:S(2)}) copy-start(s32[72,5]{0,1:T(8,128)} %param.8) | copy-start | bytes 4324
  122.8 11.9 %copy-start = (f32[16,128,128]{2,1,0:T(8,128)S(1)}, f32[16,128,128]{2,1,0:T(8,128)}, u32[]{:S(2)}) copy-start(f32[16,128,128]{2,1,0:T(8,128)} %get-tuple-element.15.st_ref) | copy-start | bytes 3145732
  122.8 11.9 %copy-start.1 = (f32[128,128]{1,0:T(8,128)S(1)}, f32[128,128]{1,0:T(8,128)}, u32[]{:S(2)}) copy-start(f32[128,128]{1,0:T(8,128)} %get-tuple-element.14.linv_ref) | copy-start | bytes 196612
